TPU v7x, 512 devices: a whole 4x4x16 slice. The times are simulated.
512 devices in a mesh: src: 32 (over x, y, z_hi), tgt: 16 (over z_lo, core).
Axes of the slice: x: 4, y: 4, z: 16 (z_hi: 2, z_lo: 8; z = z_hi * 8 + z_lo), core: 2. Of those that a mesh axis runs over, the one named last changes fastest.
Arguments:
- points_src: float32 [32768, 128], P(('src', 'tgt')), may hold values from -7 to 7
- points_tgt: float32 [8192, 128], P('tgt'), may hold values from -2 to 2
- log_source: float32 [32768], P(('src', 'tgt')), may hold values from -3 to 5.2
- log_target: float32 [8192], P('tgt'), may hold values from -3 to 3
- target_potential: float32 [8192], P('tgt'), may hold values from -4 to 60
Outputs:
- source_potential: float32 [32768], P(('src', 'tgt'))
- target_new: float32 [8192], P('tgt')
- mapped: float32 [32768, 128], P(('src', 'tgt'))
All inputs are finite; a program needn't handle non-finite values.
Results may differ from a plain program's by a relative error of at most 0.0003.
Values sent between devices are 32-bit elements; how exact they have to be, the bound alone decides.
A program may use at most 64 MiB of HBM per device.

v0:
```python
import jax
import jax.numpy as jnp
from jax import lax
from jax.sharding import PartitionSpec as P

epsilon = 0.5
floor_value = -1e30


def pair_cost(rows_a, rows_b):
    cross = jnp.dot(
        rows_a, rows_b.T, precision=lax.Precision.HIGHEST, preferred_element_type=jnp.float32
    )
    left = 0.5 * jnp.sum(rows_a * rows_a, axis=1)
    right = 0.5 * jnp.sum(rows_b * rows_b, axis=1)
    return left[:, None] + right[None, :] - cross


def row_part(rows, cols, col_pot):
    scores = (col_pot[None, :] - pair_cost(rows, cols)) / epsilon
    peak = jnp.max(scores, axis=1)
    return (peak, jnp.sum(jnp.exp(scores - peak[:, None]), axis=1))


def col_part(rows, row_pot, cols):
    scores = (row_pot[:, None] - pair_cost(rows, cols)) / epsilon
    peak = jnp.max(scores, axis=0)
    return (peak, jnp.sum(jnp.exp(scores - peak[None, :]), axis=0))


def map_part(rows, cols, col_pot):
    scores = (col_pot[None, :] - pair_cost(rows, cols)) / epsilon
    peak = jnp.max(scores, axis=1)
    weights = jnp.exp(scores - peak[:, None])
    summed = jnp.dot(
        weights, cols, precision=lax.Precision.HIGHEST, preferred_element_type=jnp.float32
    )
    return (peak, jnp.sum(weights, axis=1), summed)


def fold_pair(first, second):
    peak = jnp.maximum(first[0], second[0])
    return (peak, second[1] * jnp.exp(second[0] - peak))


def fold_triple(first, second):
    peak = jnp.maximum(first[0], second[0])
    scale_b = jnp.exp(second[0] - peak)
    return (peak, second[1] * scale_b, second[2] * scale_b[:, None])


def shards(points_src, points_tgt, log_source, log_target, target_potential):
    rows = points_src.shape[0]
    width = points_src.shape[1]
    targets = points_tgt.shape[0]
    start_rows = (jnp.full((rows,), floor_value, jnp.float32), jnp.zeros((rows,), jnp.float32))
    start_map = (
        jnp.full((rows,), floor_value, jnp.float32),
        jnp.zeros((rows,), jnp.float32),
        jnp.zeros((rows, width), jnp.float32),
    )
    piece = (
        lax.all_gather(points_tgt, "tgt", axis=0, tiled=True),
        lax.all_gather(target_potential, "tgt", axis=0, tiled=True),
    )
    peak, total = fold_pair(start_rows, row_part(points_src, piece[0], piece[1]))
    source_potential = epsilon * (log_source - peak - jnp.log(total))
    start_cols = (
        jnp.full((targets,), floor_value, jnp.float32),
        jnp.zeros((targets,), jnp.float32),
    )
    piece = (
        lax.all_gather(points_src, "tgt", axis=0, tiled=True),
        lax.all_gather(source_potential, "tgt", axis=0, tiled=True),
    )
    col_peak, col_total = fold_pair(start_cols, col_part(piece[0], piece[1], points_tgt))
    whole_peak = lax.pmax(col_peak, "src")
    whole_total = lax.psum(col_total * jnp.exp(col_peak - whole_peak), "src")
    target_new = epsilon * (log_target - whole_peak - jnp.log(whole_total))
    piece = (
        lax.all_gather(points_tgt, "tgt", axis=0, tiled=True),
        lax.all_gather(target_new, "tgt", axis=0, tiled=True),
    )
    map_peak, map_total, map_sum = fold_triple(start_map, map_part(points_src, piece[0], piece[1]))
    mapped = map_sum / map_total[:, None]
    return (source_potential, target_new, mapped)


def solution(mesh):
    return jax.shard_map(
        shards,
        mesh=mesh,
        in_specs=(P(("src", "tgt"), None), P("tgt", None), P(("src", "tgt")), P("tgt"), P("tgt")),
        out_specs=(P(("src", "tgt")), P("tgt"), P(("src", "tgt"), None)),
        check_vma=False,
    )
```

profile of v0, /device:TPU:1, one launch (start us, length us, event | category | flops | bytes accessed | tf_op | source)
XLA Modules:
  0.0 528.7 jit_solution(15344286621919854444)
XLA Ops:
  7.2 0.0 all-gather.4.cloned.1.call-start
  7.2 0.7 all-gather.4.cloned.1.call-update
  7.9 1.3 dynamic-slice
  9.8 38.1 %all-gather = f32[16,1,512]{2,1,0:T(1,128)S(1)} all-gather(f32[1,1,512]{2,1,0:T(1,128)} %bitcast.16), channel_id=1, replica_groups=mesh['src'=32,'tgt'=16] {'tgt'}, dimensions={0}, use_global_device_ids=true | all-gather | bytes 34816 | tf_op jit(solution)/shard_map/all_gather | solution.py:64
  47.9 0.9 multiply_reduce_fusion.3
  48.8 1.1 multiply_reduce_fusion.2
  49.9 28.2 %all_gather.19 = f32[1024,128]{1,0:T(8,128)S(1)} all-gather(f32[64,128]{1,0:T(8,128)} %param.5), channel_id=1, replica_groups=mesh['src'=32,'tgt'=16] {'tgt'}, dimensions={0}, use_global_device_ids=true | all-gather | bytes 557056 | tf_op jit(solution)/shard_map/all_gather | solution.py:73
  78.0 0.2 multiply_reduce_fusion.1
  78.3 0.0 copy-start.3
  78.3 41.7 %all-gather.4.cloned.1.call-done = f32[8192,128]{1,0:T(8,128)} async-done(((f32[512,128]{1,0:T(8,128)}), f32[8192,128]{1,0:T(8,128)}) %all-gather.4.cloned.1.call-update) | async-done | bytes 4194320 | tf_op jit(solution)/shard_map/all_gather | solution.py:63
  120.0 3.5 multiply_reduce_fusion
  123.5 0.0 copy-done.3
  123.5 0.0 copy-done
  123.5 4.7 fusion
  128.3 0.0 copy-start.6
  128.3 0.0 copy-start.2
  128.3 0.6 exponential_reduce_fusion.1
  128.9 0.1 copy-done.6
  128.9 0.5 fusion.16
  129.5 47.5 %all-reduce = f32[1024]{0:T(1024)S(1)} all-reduce(f32[1024]{0:T(1024)S(1)} %get-tuple-element.3), channel_id=1, replica_groups=mesh['src'=32,'tgt'=16] {'tgt'}, use_global_device_ids=true, to_apply=%add | all-reduce | flops 1024 | bytes 8192
  177.0 0.0 copy-done.2
  177.0 2.1 fusion.18
  179.0 0.4 exponential_reduce_fusion
  179.4 145.9 %pmax.7 = f32[512]{0:T(512)S(1)} all-reduce(f32[512]{0:T(512)S(1)} %broadcast_maximum_fusion), channel_id=1, replica_groups=mesh['src'=32,'tgt'=16] {'src'}, use_global_device_ids=true, to_apply=%region_7.0 | all-reduce | flops 512 | bytes 4096 | tf_op jit(solution)/shard_map/pmax | solution.py:77
  325.3 133.3 %psum.7 = f32[512]{0:T(512)S(1)} all-reduce(f32[512]{0:T(512)S(1)} %exponential_multiply_fusion), channel_id=1, replica_groups=mesh['src'=32,'tgt'=16] {'src'}, use_global_device_ids=true, to_apply=%region_9.0 | all-reduce | flops 512 | bytes 4096 | tf_op jit(solution)/shard_map/psum | solution.py:78
  458.5 0.0 copy-done.5
  458.6 57.4 %all-gather.1 = f32[16,1,512]{2,1,0:T(1,128)S(1)} all-gather(f32[1,1,512]{2,1,0:T(1,128)S(1)} %bitcast.15), channel_id=1, replica_groups=mesh['src'=32,'tgt'=16] {'tgt'}, dimensions={0}, use_global_device_ids=true | all-gather | bytes 34816 | tf_op jit(solution)/shard_map/all_gather | solution.py:82
  516.0 0.3 fusion.1
  516.3 0.6 fusion.2
  516.9 0.0 copy-done.4
  516.9 1.2 copy-done.1
  518.2 3.7 fusion.5
  (13 shorter events, 0.1 us)
Async XLA Ops:
  7.2 112.9 %all-gather.4.cloned.1.call-start = ((), (), s32[]{:S(2)}) async-start(), calls=%async_computation | async-start | bytes 4456448 | tf_op jit(solution)/shard_map/all_gather | solution.py:63
  78.3 45.3 %copy-start.3 = (f32[64,128]{1,0:T(8,128)S(1)}, f32[64,128]{1,0:T(8,128)}, u32[]{:S(2)}) copy-start(f32[64,128]{1,0:T(8,128)} %param.5) | copy-start | bytes 98308
  120.0 3.5 copy-start
  128.3 0.7 copy-start.6
  128.3 48.7 %copy-start.2 = (f32[512,128]{1,0:T(8,128)S(1)}, f32[512,128]{1,0:T(8,128)}, u32[]{:S(2)}) copy-start(f32[512,128]{1,0:T(8,128)} %param.6) | copy-start | bytes 786436
  177.0 281.6 %copy-start.5 = (f32[512]{0:T(512)S(1)}, f32[512]{0:T(512)}, u32[]{:S(2)}) copy-start(f32[512]{0:T(512)} %param.8) | copy-start | bytes 6148
  458.6 58.4 %copy-start.4 = (f32[512]{0:T(512)}, f32[512]{0:T(512)S(1)}, u32[]{:S(2)}) copy-start(f32[512]{0:T(512)S(1)} %subtract_multiply_fusion.3) | copy-start | bytes 6148
  516.0 2.2 copy-start.1
Sparse Core Ops, SparseCore 0:
  10.1 109.8 all-gather.3
where the time goes:
time: 529 us
  blocking collectives  450 us (85%)
  waiting for transfers between devices  42.4 us (8%)
  between operations  14.8 us (3%)
  matrix products  10.5 us (2%)
  other arithmetic  8.08 us (2%)
    pmax x1, blocking collectives, shards(): whole_peak = lax.pmax(col_peak, 'src')  146 us
    psum x1, blocking collectives, shards(): whole_total = lax.psum(col_total * jnp.exp(col_peak - whole_peak), 'src')  133 us
    all_gather x1, blocking collectives, shards(): lax.all_gather(target_new, 'tgt', axis=0, tiled=True)  57.4 us
    unnamed x1, blocking collectives  47.5 us
    all_gather x1, waiting for transfers between devices, shards(): lax.all_gather(points_tgt, 'tgt', axis=0, tiled=True)  41.7 us
    all_gather x1, blocking collectives, shards(): lax.all_gather(target_potential, 'tgt', axis=0, tiled=True)  38.1 us
    all_gather x1, blocking collectives, shards(): lax.all_gather(points_src, 'tgt', axis=0, tiled=True)  28.2 us
  transfers between devices with their start and end apart: 1, of which 1 were waited for; matrix products, arithmetic and copies ran while one was open for 1% of the time, Pallas kernels for 0%

commit v1 on v0

v1 whole, which is shorter than its diff:
```python
import jax
import jax.numpy as jnp
from jax import lax
from jax.experimental import pallas as pl
from jax.experimental.pallas import tpu as pltpu
from jax.sharding import PartitionSpec as P

MESH = pl.DeviceIdType.MESH
F32 = jnp.float32
BF16 = jnp.bfloat16
ROWS = 64
SLICE = 32
PLANE = 16
NEAR = (3, -3, 2, -2, 1, -1)


def lse0(values):
    peak = jnp.max(values, axis=0, keepdims=True)
    return peak + jnp.log(jnp.sum(jnp.exp(values - peak), axis=0, keepdims=True))


def kernel(
    ps, pt, ls, lt, gp,
    out_f, out_t, out_m,
    xs, tb, y2, yt, aa, ltb, sc, rb, uu, lsum, cl, cb, vv, mp, tn, mm, mb, wt,
    xs_s, xs_r, tb_s, tb_r, rb_s, rb_r, cb_s, cb_r, tn_s, tn_r, mb_s, mb_r,
):
    s = lax.axis_index("src")
    t = lax.axis_index("tgt")
    q = s // 2
    zh = s % 2
    zl = t // 2
    c = t % 2
    z = zh * 8 + zl
    x = q // 4
    y = q % 4
    me = z * 2 + c

    def plane_index(k):
        return ((x + k // 4) % 4) * 4 + (y + k % 4) % 4

    def plane_device(p):
        return (p * 2 + zh, t)

    def column_device(to_z, to_c):
        return (q * 2 + to_z // 8, (to_z % 8) * 2 + to_c)

    def plane_copy(src, dst, send, recv, p, slot):
        return pltpu.make_async_remote_copy(
            src_ref=src, dst_ref=dst, send_sem=send.at[p], recv_sem=recv.at[slot],
            device_id=plane_device(p), device_id_type=MESH,
        )

    def column_copy(buf, slot, send, recv, k, to_z, to_c):
        return pltpu.make_async_remote_copy(
            src_ref=buf.at[slot], dst_ref=buf.at[slot], send_sem=send.at[k], recv_sem=recv.at[slot],
            device_id=column_device(to_z, to_c), device_id_type=MESH,
        )

    barrier = pltpu.get_barrier_semaphore()

    def greet_column(k, carry):
        pl.semaphore_signal(
            barrier, inc=1, device_id=column_device((z + k // 2) % 16, (c + k % 2) % 2), device_id_type=MESH
        )
        return carry

    def greet_plane(k, carry):
        pl.semaphore_signal(barrier, inc=1, device_id=plane_device(plane_index(k)), device_id_type=MESH)
        return carry

    lax.fori_loop(1, 32, greet_column, 0)
    lax.fori_loop(1, PLANE, greet_plane, 0)

    xs[pl.ds(q, 1)] = ps[...][None]
    tb[pl.ds(t, 1), 0:SLICE] = pt[pl.ds(q * SLICE, SLICE), :][None]
    tb[pl.ds(t, 1), SLICE : SLICE + 1] = gp[pl.ds(q // 4, 1), :][None]
    tb[pl.ds(t, 1), SLICE + 1 : SLICE + 2] = lt[pl.ds(q // 4, 1), :][None]

    pl.semaphore_wait(barrier, 31 + 15)

    far = 4 - 8 * c
    target_sends = []
    for d in (far,) + NEAR:
        for to_c in range(2):
            target_sends.append(column_copy(tb, t, tb_s, tb_r, len(target_sends), (z + d + 16) % 16, to_c))
    target_sends.append(column_copy(tb, t, tb_s, tb_r, len(target_sends), z, 1 - c))
    for copy in target_sends:
        copy.start()

    def send_points(k, carry):
        p = plane_index(16 - k)
        plane_copy(xs.at[q], xs.at[q], xs_s, xs_r, p, q).start()
        return carry

    lax.fori_loop(1, PLANE, send_points, 0)

    sq = jnp.concatenate([ps[...] * ps[...], jnp.zeros((128 - ROWS, 128), F32)], axis=0)
    norm = jnp.sum(sq.T, axis=0, keepdims=True)

    lane = lax.broadcasted_iota(jnp.int32, (SLICE, 128), 1)
    sub = lax.broadcasted_iota(jnp.int32, (SLICE, 128), 0)
    mine = lane == sub + (q % 4) * SLICE

    def take_targets(k, carry):
        e = k // 2
        half = (e + 1) // 2
        off = (e % 2) * half + (1 - e % 2) * ((8 - half) % 8)
        slot = ((zl + off) % 8) * 2 + k % 2

        @pl.when(slot != t)
        def _():
            column_copy(tb, slot, tb_s, tb_r, 0, z, 1 - c).wait_recv()

        pts = tb[pl.ds(slot, 1), 0:SLICE][0]
        grow = tb[pl.ds(slot, 1), SLICE : SLICE + 1][0]
        lrow = tb[pl.ds(slot, 1), SLICE + 1 : SLICE + 2][0]
        rows = pl.ds(pl.multiple_of(slot * SLICE, SLICE), SLICE)
        a = jnp.sum(jnp.where(mine, 2.0 * grow, 0.0) - pts * pts, axis=1, keepdims=True)
        l = jnp.sum(jnp.where(mine, lrow, 0.0), axis=1, keepdims=True)
        aa[rows, :] = jnp.broadcast_to(a, (SLICE, 128))
        ltb[rows, :] = jnp.broadcast_to(l, (SLICE, 128))
        y2[rows, :] = 2.0 * pts
        return carry

    lax.fori_loop(0, 16, take_targets, 0)
    for b in range(4):
        yb = 0.5 * y2[b * 128 : (b + 1) * 128, :].T
        hi = yb.astype(BF16)
        yt[0:128, b * 128 : (b + 1) * 128] = hi
        yt[128:256, b * 128 : (b + 1) * 128] = (yb - hi.astype(F32)).astype(BF16)

    def pair_at(m, b):
        a = m + (m // 2) * (5 - 2 * m)
        return ((x + a) % 4) * 2 + (y // 2 + b) % 2

    def take_sources(k, carry):
        pair = pair_at(k // 2, k % 2)
        for h in range(2):
            p = 2 * pair + h

            @pl.when(p != q)
            def _():
                plane_copy(xs.at[p], xs.at[p], xs_s, xs_r, p, p).wait_recv()

        pts = xs[pl.ds(2 * pair, 2)].reshape(128, 128)
        prod = lax.dot_general(
            y2[...], pts, (((1,), (1,)), ((), ())),
            precision=lax.Precision.HIGHEST, preferred_element_type=F32,
        )
        score = prod + aa[...]
        sc[pl.ds(pair, 1)] = score[None]
        rb[pl.ds(q, 1), pl.ds(pair, 1)] = lse0(score)[None]
        return carry

    lax.fori_loop(0, 8, take_sources, 0)
    half = lax.broadcasted_iota(jnp.int32, (1, 128), 1) // 64 == q % 2
    both = jnp.concatenate([ls[...], ls[...]], axis=1)
    rb[pl.ds(q, 1), 8:9] = jnp.where(half, both, 0.0)[None]

    def send_rows(k, carry):
        p = plane_index(16 - k)
        plane_copy(rb.at[q], rb.at[q], rb_s, rb_r, p, q).start()
        return carry

    lax.fori_loop(1, PLANE, send_rows, 0)

    def wait_rows(k, carry):
        p = plane_index(k)
        plane_copy(rb.at[p], rb.at[p], rb_s, rb_r, p, p).wait_recv()
        return carry

    lax.fori_loop(1, PLANE, wait_rows, 0)
    part = rb[:, 0:8]
    rowlse = lse0(part)[0]
    uu[...] = rowlse
    for b in range(8):
        lsum[b : b + 1, :] = rb[2 * b, 8:9] + rb[2 * b + 1, 8:9]

    own_lse = uu[pl.ds(q // 2, 1), :]
    own_lse = jnp.where(q % 2 == 0, own_lse, pltpu.roll(own_lse, 64, 1))
    out_f[...] = 0.5 * (ls[...] + norm[:, 0:ROWS] - own_lse[:, 0:ROWS])
    u = lsum[...] - rowlse

    def columns(j, carry):
        rows = pl.ds(pl.multiple_of(j * 32, 32), 32)
        vals = [u[b : b + 1, :] + sc[b, rows, :] for b in range(8)]
        peak = vals[0]
        for v in vals[1:]:
            peak = jnp.maximum(peak, v)
        total = jnp.exp(vals[0] - peak)
        for v in vals[1:]:
            total = total + jnp.exp(v - peak)
        cl[rows, :] = peak + jnp.log(total)
        return carry

    lax.fori_loop(0, 16, columns, 0)
    for b in range(4):
        cb[pl.ds(me, 1), b : b + 1] = lse0(cl[b * 128 : (b + 1) * 128, :].T)[None]

    def send_columns(k, carry):
        m = k // 2
        near = (m + 1) // 2
        d = (8 - near) * (1 - m % 2) + (8 + near) * (m % 2)
        column_copy(cb, me, cb_s, cb_r, k, (z + d) % 16, k % 2).start()
        return carry

    lax.fori_loop(0, 30, send_columns, 0)
    column_copy(cb, me, cb_s, cb_r, 30, z, 1 - c).start()

    def wait_columns(k, carry):
        slot = (me + k) % 32
        column_copy(cb, slot, cb_s, cb_r, 0, z, 1 - c).wait_recv()
        return carry

    lax.fori_loop(1, 32, wait_columns, 0)
    collse = lse0(cb[...])[0]
    for b in range(4):
        mp[b] = collse[b : b + 1, :]
        spread = jnp.broadcast_to(collse[b : b + 1, :], (128, 128)).T
        vv[b * 128 : (b + 1) * 128, :] = ltb[b * 128 : (b + 1) * 128, :] - spread
    tn[pl.ds(q, 1)] = mp[pl.ds(t // 4, 1)]

    def send_new(k, carry):
        p = plane_index(16 - k)
        plane_copy(tn.at[q], tn.at[q], tn_s, tn_r, p, q).start()
        return carry

    lax.fori_loop(1, PLANE, send_new, 0)

    def map_pair(k, carry):
        pair = pair_at(3 - k // 2, 1 - k % 2)
        val = vv[...] + sc[pl.ds(pair, 1)][0]
        peak = jnp.max(val, axis=0, keepdims=True)
        w = jnp.exp(val - peak)
        total = jnp.sum(w, axis=0, keepdims=True)
        hi = w.astype(BF16)
        lo = (w - hi.astype(F32)).astype(BF16)
        first = jnp.dot(yt[...], hi, preferred_element_type=F32)
        second = jnp.dot(yt[0:128, :], lo, preferred_element_type=F32)
        n = (first[0:128] + first[128:256] + second).T
        for h in range(2):
            p = 2 * pair + h
            mm[pl.ds(p, 1), 0:ROWS] = n[h * ROWS : (h + 1) * ROWS][None]
            mm[pl.ds(p, 1), ROWS : ROWS + 1] = peak[None]
            mm[pl.ds(p, 1), ROWS + 1 : ROWS + 2] = total[None]

            @pl.when(p != q)
            def _():
                plane_copy(mm.at[p], mb.at[q], mb_s, mb_r, p, q).start()

        return carry

    lax.fori_loop(0, 8, map_pair, 0)
    mb[pl.ds(q, 1)] = mm[pl.ds(q, 1)]

    def wait_new(k, carry):
        p = plane_index(k)
        plane_copy(tn.at[p], tn.at[p], tn_s, tn_r, p, p).wait_recv()
        return carry

    lax.fori_loop(1, PLANE, wait_new, 0)
    pieces = tn[...].reshape(16, 128)
    lane16 = lax.broadcasted_iota(jnp.int32, (16, 128), 1) // SLICE
    sub16 = lax.broadcasted_iota(jnp.int32, (16, 128), 0) % 4
    whole = jnp.zeros((16, 128), F32)
    for k in range(4):
        turned = pltpu.roll(pieces, ((k - t % 4 + 4) % 4) * SLICE, 1)
        whole = whole + jnp.where((lane16 == k) & (sub16 == k), turned, 0.0)
    for b in range(4):
        row = jnp.sum(whole[4 * b : 4 * b + 4], axis=0, keepdims=True)
        out_t[b : b + 1, :] = gp[b : b + 1, :] + 0.5 * (lt[b : b + 1, :] - row)

    def wait_map(k, carry):
        p = plane_index(k)
        plane_copy(mm.at[p], mb.at[p], mb_s, mb_r, p, p).wait_recv()
        return carry

    lax.fori_loop(1, PLANE, wait_map, 0)
    peaks = jnp.concatenate([mb[p, ROWS : ROWS + 1] for p in range(16)], axis=0)
    totals = jnp.concatenate([mb[p, ROWS + 1 : ROWS + 2] for p in range(16)], axis=0)
    scale = jnp.exp(peaks - jnp.max(peaks, axis=0, keepdims=True))
    scale = scale / jnp.sum(scale * totals, axis=0, keepdims=True)
    wt[...] = jnp.concatenate([scale, jnp.zeros((112, 128), F32)], axis=0).T
    weights = wt[pl.ds(pl.multiple_of((q % 2) * ROWS, ROWS), ROWS), :]
    total = weights[:, 0:1] * mb[0, 0:ROWS]
    for p in range(1, 16):
        total = total + weights[:, p : p + 1] * mb[p, 0:ROWS]
    out_m[...] = total

    for copy in target_sends:
        copy.wait_send()

    def sent_plane(k, carry):
        p = plane_index(k)
        plane_copy(xs.at[q], xs.at[q], xs_s, xs_r, p, q).wait_send()
        plane_copy(rb.at[q], rb.at[q], rb_s, rb_r, p, q).wait_send()
        plane_copy(tn.at[q], tn.at[q], tn_s, tn_r, p, q).wait_send()
        plane_copy(mm.at[p], mb.at[q], mb_s, mb_r, p, q).wait_send()
        return carry

    lax.fori_loop(1, PLANE, sent_plane, 0)

    def sent_columns(k, carry):
        column_copy(cb, me, cb_s, cb_r, k, z, 1 - c).wait_send()
        return carry

    lax.fori_loop(0, 31, sent_columns, 0)


def shards(points_src, points_tgt, log_source, log_target, target_potential):
    vmem = pl.BlockSpec(memory_space=pltpu.VMEM)
    dma = pltpu.SemaphoreType.DMA
    source_potential, target_new, mapped = pl.pallas_call(
        kernel,
        name="sinkhorn",
        out_shape=(
            jax.ShapeDtypeStruct((1, ROWS), F32),
            jax.ShapeDtypeStruct((4, 128), F32),
            jax.ShapeDtypeStruct((ROWS, 128), F32),
        ),
        in_specs=[vmem] * 5,
        out_specs=(vmem,) * 3,
        scratch_shapes=[
            pltpu.VMEM((16, ROWS, 128), F32),
            pltpu.VMEM((16, 40, 128), F32),
            pltpu.VMEM((512, 128), F32),
            pltpu.VMEM((256, 512), BF16),
            pltpu.VMEM((512, 128), F32),
            pltpu.VMEM((512, 128), F32),
            pltpu.VMEM((8, 512, 128), F32),
            pltpu.VMEM((16, 16, 128), F32),
            pltpu.VMEM((8, 128), F32),
            pltpu.VMEM((8, 128), F32),
            pltpu.VMEM((512, 128), F32),
            pltpu.VMEM((32, 4, 128), F32),
            pltpu.VMEM((512, 128), F32),
            pltpu.VMEM((4, 1, 128), F32),
            pltpu.VMEM((16, 1, 128), F32),
            pltpu.VMEM((16, 72, 128), F32),
            pltpu.VMEM((16, 72, 128), F32),
            pltpu.VMEM((128, 128), F32),
            dma((16,)), dma((16,)),
            dma((16,)), dma((16,)),
            dma((16,)), dma((16,)),
            dma((32,)), dma((32,)),
            dma((16,)), dma((16,)),
            dma((16,)), dma((16,)),
        ],
        compiler_params=pltpu.CompilerParams(
            collective_id=0, has_side_effects=True, vmem_limit_bytes=40 * 2**20
        ),
    )(
        points_src,
        points_tgt,
        log_source.reshape(1, ROWS),
        log_target.reshape(4, 128),
        target_potential.reshape(4, 128),
    )
    return source_potential.reshape(ROWS), target_new.reshape(512), mapped


def solution(mesh):
    return jax.shard_map(
        shards,
        mesh=mesh,
        in_specs=(P(("src", "tgt"), None), P("tgt", None), P(("src", "tgt")), P("tgt"), P("tgt")),
        out_specs=(P(("src", "tgt")), P("tgt"), P(("src", "tgt"), None)),
        check_vma=False,
    )
```

time: 529 us -> 63.9 us (0.12)
  blocking collectives: 450 us -> 0 us
  Pallas kernels: 0 us -> 58.9 us
  waiting for transfers between devices: 42.4 us -> 0 us
  between operations: 14.8 us -> 0.67 us
  matrix products: 10.5 us -> 0 us
  other arithmetic: 8.08 us -> 0 us
    pmax x1 -> x0, blocking collectives: 146 us -> none  [shards(): whole_peak = lax.pmax(col_peak, 'src')]
    psum x1 -> x0, blocking collectives: 133 us -> none  [shards(): whole_total = lax.psum(col_total * jnp.exp(col_peak - whole_peak), 'src')]
    all_gather x3 -> x0, blocking collectives: 124 us -> none  [the longest x1 57.4 us: shards(): lax.all_gather(target_new, 'tgt', axis=0, tiled=True)]
    pallas_call x0 -> x1, Pallas kernels: none -> 58.9 us  [shards(): pl.pallas_call(kernel, name='sinkhorn', out_shape=(jax.ShapeDtypeStruct((...]
    unnamed x1 -> x0, blocking collectives: 47.5 us -> none
    all_gather x1 -> x0, waiting for transfers between devices: 41.7 us -> none  [shards(): lax.all_gather(points_tgt, 'tgt', axis=0, tiled=True)]
    dot_general x3 -> x0, matrix products: 10.5 us -> none  [the longest x2 6.77 us: pair_cost(): jnp.dot(rows_a, rows_b.T, precision=lax.Precision.HIGHEST, preferred_elem...]
    reduce_sum x7 -> x0, other arithmetic: 7.18 us -> none  [the longest x2 4.59 us: pair_cost(): right = 0.5 * jnp.sum(rows_b * rows_b, axis=1)]
  transfers between devices with their start and end apart: 1 -> 0, of which waited for: 1 -> 0; matrix products, arithmetic and copies ran while one was open for 1% -> 0% of each run, Pallas kernels for 0% -> 0%
where the time goes in v1:
time: 63.9 us; the launch traced here: 63.6 us
  Pallas kernels  58.9 us (92%)
  local copies, waits for them, and re-layouts  4.09 us (6%)
  between operations  0.67 us (1%)
    pallas_call x1, Pallas kernels, shards(): pl.pallas_call(kernel, name='sinkhorn', out_shape=(jax.ShapeDtypeStruct((...  58.9 us
    unnamed x13, local copies, waits for them, and re-layouts  4.09 us

profile of v1, /device:TPU:1, one launch (start us, length us, event | category | flops | bytes accessed | tf_op | source)
XLA Modules:
  0.0 63.6 jit_solution(7190489731452595407)
XLA Ops:
  0.6 0.0 copy-start.3
  0.6 0.0 copy-start.2
  0.7 0.0 copy-start.4
  0.7 0.7 %copy-done.3 = f32[512]{0:T(512)S(1)} copy-done((f32[512]{0:T(512)S(1)}, f32[512]{0:T(512)}, u32[]{:S(2)}) %copy-start.3) | copy-done | bytes 2072
  1.3 0.0 copy-done.2
  1.3 0.0 copy-done.4
  1.3 0.0 copy-start
  1.3 0.9 %copy-done = f32[512,128]{1,0:T(8,128)S(1)} copy-done((f32[512,128]{1,0:T(8,128)S(1)}, f32[512,128]{1,0:T(8,128)}, u32[]{:S(2)}) %copy-start) | copy-done | bytes 262168
  2.3 0.0 copy-start.1
  2.3 0.8 %copy-done.1 = f32[64,128]{1,0:T(8,128)S(1)} copy-done((f32[64,128]{1,0:T(8,128)S(1)}, f32[64,128]{1,0:T(8,128)}, u32[]{:S(2)}) %copy-start.1) | copy-done | bytes 32792
  3.0 58.9 %sinkhorn.1 = (f32[1,64]{1,0:T(1,128)S(1)}, f32[4,128]{1,0:T(4,128)S(1)}, f32[64,128]{1,0:T(8,128)S(1)}) custom-call(f32[64,128]{1,0:T(8,128)S(1)} %copy-done.1, f32[512,128]{1,0:T(8,128)S(1)} %copy-done, f32[1,64]{1,0:T(1,128)S(1)} %bitcast.8, f32[4,128]{1,0:T(4,128)S(1)} %bitcast.5, f32[4,128]{1,0:T(4,128)S(1)} %bitcast.6), custom_call_target="tpu_custom_call" | custom-call | tf_op jit(solution)/shard_map/sinkhorn/pallas_call | solution.py:314
  61.9 0.5 copy.11
  62.4 0.6 copy.12
  63.0 0.6 copy.13
Async XLA Ops:
  0.6 0.7 %copy-start.3 = (f32[512]{0:T(512)S(1)}, f32[512]{0:T(512)}, u32[]{:S(2)}) copy-start(f32[512]{0:T(512)} %param.9) | copy-start | bytes 6148
  0.6 0.7 %copy-start.2 = (f32[512]{0:T(512)S(1)}, f32[512]{0:T(512)}, u32[]{:S(2)}) copy-start(f32[512]{0:T(512)} %param.8) | copy-start | bytes 6148
  0.7 0.7 %copy-start.4 = (f32[64]{0:T(128)S(1)}, f32[64]{0:T(128)}, u32[]{:S(2)}) copy-start(f32[64]{0:T(128)} %param.7) | copy-start | bytes 772
  1.3 1.0 %copy-start = (f32[512,128]{1,0:T(8,128)S(1)}, f32[512,128]{1,0:T(8,128)}, u32[]{:S(2)}) copy-start(f32[512,128]{1,0:T(8,128)} %pt.1) | copy-start | bytes 786436
  2.3 0.8 %copy-start.1 = (f32[64,128]{1,0:T(8,128)S(1)}, f32[64,128]{1,0:T(8,128)}, u32[]{:S(2)}) copy-start(f32[64,128]{1,0:T(8,128)} %ps.1) | copy-start | bytes 98308

commit v2 on v0

v2 whole, which is shorter than its diff:
```python
import jax
import jax.numpy as jnp
from jax import lax
from jax.experimental import pallas as pl
from jax.experimental.pallas import tpu as pltpu
from jax.sharding import PartitionSpec as P

MESH = pl.DeviceIdType.MESH
F32 = jnp.float32
BF16 = jnp.bfloat16
ROWS = 64
SLICE = 32
QUAD = 4 * ROWS


def ring(a):
    return min(a, 4 - a)


PEERS = sorted(((a, b) for a in range(4) for b in range(4) if a or b), key=lambda o: -ring(o[0]) - ring(o[1]))
NEAR = (3, -3, 2, -2, 1, -1)


def lse0(values):
    peak = jnp.max(values, axis=0, keepdims=True)
    return peak + jnp.log(jnp.sum(jnp.exp(values - peak), axis=0, keepdims=True))


def split3(v):
    hi = v.astype(BF16)
    rest = v - hi.astype(F32)
    mid = rest.astype(BF16)
    return hi, mid, (rest - mid.astype(F32)).astype(BF16)


def kernel(
    ps, pt, ls, lt, gp,
    out_f, out_t, out_m,
    xs, tb, gv, lv, lsv, y1, y3, yf, yt, aa, ltb, sc, rb, uu, lsum, cl, cb, vv, mp, tn, mm, mb, wt,
    loc, xs_s, xs_r, tb_s, tb_r, rb_s, rb_r, cb_s, cb_r, tn_s, tn_r, mb_s, mb_r,
):
    s = lax.axis_index("src")
    t = lax.axis_index("tgt")
    q = s >> 1
    zl = t >> 1
    c = t & 1
    z = (s & 1) * 8 + zl
    x = q >> 2
    y = q & 3
    me = z * 2 + c

    def peer(a, b):
        return ((x + a) & 3) * 4 + ((y + b) & 3)

    def plane_device(p):
        return (p * 2 + (s & 1), t)

    def column_device(to_z, to_c):
        return (q * 2 + (to_z >> 3), (to_z & 7) * 2 + to_c)

    def remote(src, dst, send, recv, device):
        return pltpu.make_async_remote_copy(
            src_ref=src, dst_ref=dst, send_sem=send, recv_sem=recv, device_id=device, device_id_type=MESH
        )

    def take(ref, recv):
        remote(ref, ref, recv, recv, plane_device(peer(1, 0))).wait_recv()

    def left(ref, send):
        remote(ref, ref, send, send, plane_device(peer(1, 0))).wait_send()

    barrier = pltpu.get_barrier_semaphore()
    for d in (4, -4, 3, -3, 2, -2, 1, -1):
        for to_c in range(2):
            pl.semaphore_signal(
                barrier, inc=1, device_id=column_device((z + d) & 15, to_c), device_id_type=MESH
            )
    for a, b in PEERS:
        pl.semaphore_signal(barrier, inc=1, device_id=plane_device(peer(a, b)), device_id_type=MESH)
    pl.semaphore_signal(barrier, inc=1, device_id=column_device(z, 1 - c), device_id_type=MESH)

    local = [
        pltpu.make_async_copy(gp, gv, loc.at[0]),
        pltpu.make_async_copy(lt, lv, loc.at[1]),
        pltpu.make_async_copy(pt.at[pl.ds(pl.multiple_of(q * SLICE, SLICE), SLICE)], tb.at[t, pl.ds(0, SLICE)], loc.at[2]),
        pltpu.make_async_copy(ps, xs.at[q], loc.at[3]),
        pltpu.make_async_copy(ls, lsv, loc.at[4]),
    ]
    for copy in local:
        copy.start()
    for copy in local:
        copy.wait()
    tb[pl.ds(t, 1), SLICE : SLICE + 1] = gv[pl.ds(q >> 2, 1), :][None]
    tb[pl.ds(t, 1), SLICE + 1 : SLICE + 2] = lv[pl.ds(q >> 2, 1), :][None]

    pl.semaphore_wait(barrier, 16 + 15 + 1)

    def send_targets(d, to_c):
        remote(
            tb.at[t], tb.at[t], tb_s.at[0], tb_r.at[abs(d)],
            column_device((z + d) & 15, (1 - c) if to_c is None else to_c),
        ).start()

    def send_points(a, b):
        remote(xs.at[q], xs.at[q], xs_s.at[0], xs_r.at[x], plane_device(peer(a, b))).start()

    todo = list(PEERS)
    for to_c in range(2):
        remote(
            tb.at[t], tb.at[t], tb_s.at[0], tb_r.at[4], column_device((z + 4 - 8 * c) & 15, to_c)
        ).start()
        send_points(*todo.pop(0))
    for d in NEAR:
        for to_c in range(2):
            send_targets(d, to_c)
            send_points(*todo.pop(0))
    send_points(*todo.pop(0))
    send_targets(0, None)

    lane = lax.broadcasted_iota(jnp.int32, (SLICE, 128), 1)
    sub = lax.broadcasted_iota(jnp.int32, (SLICE, 128), 0)
    mine = lane == sub + (q & 3) * SLICE

    def use_targets(off):
        for to_c in range(2):
            slot = ((zl + off) & 7) * 2 + to_c
            block = tb[pl.ds(slot, 1)][0]
            pts = block[0:SLICE]
            rows = pl.ds(pl.multiple_of(slot * SLICE, SLICE), SLICE)
            own = jnp.where(mine, 2.0 * block[SLICE : SLICE + 1], 0.0)
            a = jnp.sum(own - pts * pts, axis=1, keepdims=True)
            aa[rows, :] = jnp.broadcast_to(a, (SLICE, 128))
            hi, mid, lo = split3(2.0 * pts)
            yf[rows, :] = pts
            y1[rows, 0:128] = hi
            y1[rows, 128:256] = mid
            y3[rows, 0:128] = hi
            y3[rows, 128:256] = lo

    take(tb.at[0], tb_r.at[0])
    use_targets(0)
    for d in (1, 2, 3):
        take(tb.at[pl.ds(0, 4)], tb_r.at[d])
        use_targets(d)
        use_targets(8 - d)
    take(tb.at[pl.ds(0, 2)], tb_r.at[4])
    use_targets(4)

    for a in (0, 1, 3, 2):
        quad = (x + a) & 3
        take(xs.at[pl.ds(0, 4 if a else 3)], xs_r.at[quad])
        pts = xs[pl.ds(quad * 4, 4)].reshape(QUAD, 128)
        hi, mid, lo = split3(pts)

        def product(targets, first, second):
            return lax.dot_general(
                targets, jnp.concatenate([first, second], axis=1),
                (((1,), (1,)), ((), ())), preferred_element_type=F32,
            )

        prod = product(y3[...], lo, hi) + product(y1[...], mid, hi) + product(y1[...], hi, mid)
        score = prod + jnp.concatenate([aa[...], aa[...]], axis=1)
        sc[pl.ds(quad, 1)] = score[None]
        row = lse0(score)
        rb[pl.ds(q, 1), pl.ds(2 * quad, 1)] = row[:, 0:128][None]
        rb[pl.ds(q, 1), pl.ds(2 * quad + 1, 1)] = row[:, 128:256][None]

    half = (lax.broadcasted_iota(jnp.int32, (1, 128), 1) >> 6) == (q & 1)
    both = jnp.concatenate([lsv[...], lsv[...]], axis=1)
    rb[pl.ds(q, 1), 8:9] = jnp.where(half, both, 0.0)[None]
    for a, b in PEERS:
        remote(rb.at[q], rb.at[q], rb_s.at[0], rb_r.at[0], plane_device(peer(a, b))).start()

    for b in range(4):
        yb = yf[b * 128 : (b + 1) * 128, :].T
        hi = yb.astype(BF16)
        yt[0:128, b * 128 : (b + 1) * 128] = hi
        yt[128:256, b * 128 : (b + 1) * 128] = (yb - hi.astype(F32)).astype(BF16)
    for slot in range(16):
        l = jnp.sum(jnp.where(mine, tb[slot, SLICE + 1 : SLICE + 2], 0.0), axis=1, keepdims=True)
        ltb[slot * SLICE : (slot + 1) * SLICE, :] = jnp.broadcast_to(l, (SLICE, 128))
    own_points = xs[pl.ds(q, 1)][0]
    squares = jnp.concatenate([own_points * own_points, jnp.zeros((128 - ROWS, 128), F32)], axis=0)
    norm = jnp.sum(squares.T, axis=0, keepdims=True)

    take(rb.at[pl.ds(0, 15)], rb_r.at[0])
    rowlse = lse0(rb[:, 0:8])[0]
    uu[...] = rowlse
    for b in range(8):
        lsum[b : b + 1, :] = rb[2 * b, 8:9] + rb[2 * b + 1, 8:9]
    u = lsum[...] - rowlse

    def columns(j, carry):
        rows = pl.ds(pl.multiple_of(j * 32, 32), 32)
        vals = []
        for b in range(8):
            lanes = slice((b % 2) * 128, (b % 2) * 128 + 128)
            v = u[b : b + 1, :] + sc[b // 2, rows, lanes]
            sc[b // 2, rows, lanes] = v
            vals.append(v)
        peak = vals[0]
        for v in vals[1:]:
            peak = jnp.maximum(peak, v)
        total = jnp.exp(vals[0] - peak)
        for v in vals[1:]:
            total = total + jnp.exp(v - peak)
        cl[rows, :] = peak + jnp.log(total)
        return carry

    lax.fori_loop(0, 16, columns, 0)
    for b in range(4):
        cb[pl.ds(me, 1), b : b + 1] = lse0(cl[b * 128 : (b + 1) * 128, :].T)[None]

    def send_columns(d, to_c):
        remote(cb.at[me], cb.at[me], cb_s.at[0], cb_r.at[0], column_device((z + d) & 15, to_c)).start()

    for d in (8, 7, -7, 6, -6, 5, -5, 4, -4, 3, -3, 2, -2, 1, -1):
        for to_c in range(2):
            send_columns(d, to_c)
    send_columns(0, 1 - c)

    own_lse = uu[pl.ds(q >> 1, 1), :]
    own_lse = jnp.where(q & 1 == 0, own_lse, pltpu.roll(own_lse, 64, 1))
    out_f[...] = 0.5 * (lsv[...] + norm[:, 0:ROWS] - own_lse[:, 0:ROWS])

    take(cb.at[pl.ds(0, 31)], cb_r.at[0])
    collse = lse0(cb[...])[0]
    for b in range(4):
        mp[b] = collse[b : b + 1, :]
        spread = jnp.broadcast_to(collse[b : b + 1, :], (128, 128)).T
        vv[b * 128 : (b + 1) * 128, :] = ltb[b * 128 : (b + 1) * 128, :] - spread

    for a in (2, 1, 3, 0):
        quad = (x + a) & 3
        val = sc[pl.ds(quad, 1)][0] + jnp.concatenate([vv[...], vv[...]], axis=1)
        w = jnp.exp(val)
        total = jnp.sum(w, axis=0, keepdims=True)
        hi = w.astype(BF16)
        lo = (w - hi.astype(F32)).astype(BF16)
        first = jnp.dot(yt[...], hi, preferred_element_type=F32)
        second = jnp.dot(yt[0:128, :], lo, preferred_element_type=F32)
        n = first[0:128] + first[128:256] + second
        n = jnp.concatenate([n[:, 0:128].T, n[:, 128:256].T], axis=0)
        for h in range(4):
            part = jnp.concatenate([n[h * ROWS : (h + 1) * ROWS], total[:, (h // 2) * 128 : (h // 2) * 128 + 128]], axis=0)
            mm[pl.ds(quad * 4 + h, 1)] = part[None]
        for b in (2, 1, 3, 0):
            if a or b:
                p = peer(a, b)
                remote(mm.at[p], mb.at[q], mb_s.at[0], mb_r.at[x], plane_device(p)).start()

    tn[pl.ds(q, 1)] = mp[pl.ds(t >> 2, 1)]
    for a, b in PEERS:
        remote(tn.at[q], tn.at[q], tn_s.at[0], tn_r.at[0], plane_device(peer(a, b))).start()
    take(tn.at[pl.ds(0, 15)], tn_r.at[0])
    pieces = tn[...].reshape(16, 128)
    lane16 = lax.broadcasted_iota(jnp.int32, (16, 128), 1) >> 5
    sub16 = lax.broadcasted_iota(jnp.int32, (16, 128), 0) & 3
    whole = jnp.zeros((16, 128), F32)
    for k in range(4):
        turned = pltpu.roll(pieces, ((k - t) & 3) * SLICE, 1)
        whole = whole + jnp.where((lane16 == k) & (sub16 == k), turned, 0.0)
    for b in range(4):
        row = jnp.sum(whole[4 * b : 4 * b + 4], axis=0, keepdims=True)
        out_t[b : b + 1, :] = gv[b : b + 1, :] + 0.5 * (lv[b : b + 1, :] - row)

    mb[pl.ds(q, 1)] = mm[pl.ds(q, 1)]
    total = jnp.zeros((ROWS + 1, 128), F32)
    for a in (0, 1, 3, 2):
        quad = (x + a) & 3
        take(mb.at[pl.ds(0, 4 if a else 3)], mb_r.at[quad])
        got = mb[pl.ds(quad * 4, 4)]
        total = total + ((got[0] + got[1]) + (got[2] + got[3]))
    wt[...] = jnp.broadcast_to(1.0 / total[ROWS : ROWS + 1], (128, 128)).T
    out_m[...] = total[0:ROWS] * wt[pl.ds(pl.multiple_of((q & 1) * ROWS, ROWS), ROWS), :]

    left(tb.at[pl.ds(0, 15)], tb_s.at[0])
    left(xs.at[pl.ds(0, 15)], xs_s.at[0])
    left(rb.at[pl.ds(0, 15)], rb_s.at[0])
    left(cb.at[pl.ds(0, 31)], cb_s.at[0])
    left(tn.at[pl.ds(0, 15)], tn_s.at[0])
    left(mm.at[pl.ds(0, 15)], mb_s.at[0])


def finish(f_ref, t_ref, m_ref, out_f, out_t, out_m):
    out_f[...] = f_ref[...]
    out_t[...] = t_ref[...]
    out_m[...] = m_ref[...]


def shards(points_src, points_tgt, log_source, log_target, target_potential):
    vmem = pl.BlockSpec(memory_space=pltpu.VMEM)
    hbm = pl.BlockSpec(memory_space=pltpu.HBM)
    dma = pltpu.SemaphoreType.DMA
    shapes = (
        jax.ShapeDtypeStruct((1, ROWS), F32),
        jax.ShapeDtypeStruct((4, 128), F32),
        jax.ShapeDtypeStruct((ROWS, 128), F32),
    )
    results = pl.pallas_call(
        kernel,
        name="sinkhorn",
        out_shape=shapes,
        in_specs=[hbm] * 5,
        out_specs=(vmem,) * 3,
        scratch_shapes=[
            pltpu.VMEM((16, ROWS, 128), F32),
            pltpu.VMEM((16, SLICE + 2, 128), F32),
            pltpu.VMEM((4, 128), F32),
            pltpu.VMEM((4, 128), F32),
            pltpu.VMEM((1, ROWS), F32),
            pltpu.VMEM((512, 256), BF16),
            pltpu.VMEM((512, 256), BF16),
            pltpu.VMEM((512, 128), F32),
            pltpu.VMEM((256, 512), BF16),
            pltpu.VMEM((512, 128), F32),
            pltpu.VMEM((512, 128), F32),
            pltpu.VMEM((4, 512, QUAD), F32),
            pltpu.VMEM((16, 9, 128), F32),
            pltpu.VMEM((8, 128), F32),
            pltpu.VMEM((8, 128), F32),
            pltpu.VMEM((512, 128), F32),
            pltpu.VMEM((32, 4, 128), F32),
            pltpu.VMEM((512, 128), F32),
            pltpu.VMEM((4, 1, 128), F32),
            pltpu.VMEM((16, 1, 128), F32),
            pltpu.VMEM((16, ROWS + 1, 128), F32),
            pltpu.VMEM((16, ROWS + 1, 128), F32),
            pltpu.VMEM((128, 128), F32),
            dma((5,)),
            dma((1,)), dma((4,)),
            dma((1,)), dma((5,)),
            dma((1,)), dma((1,)),
            dma((1,)), dma((1,)),
            dma((1,)), dma((1,)),
            dma((1,)), dma((4,)),
        ],
        compiler_params=pltpu.CompilerParams(
            collective_id=0, has_side_effects=True, vmem_limit_bytes=56 * 2**20
        ),
    )(
        points_src,
        points_tgt,
        log_source.reshape(1, ROWS),
        log_target.reshape(4, 128),
        target_potential.reshape(4, 128),
    )
    source_potential, target_new, mapped = pl.pallas_call(
        finish, name="finish", out_shape=shapes, in_specs=[vmem] * 3, out_specs=(vmem,) * 3
    )(*results)
    return source_potential.reshape(ROWS), target_new.reshape(512), mapped


def solution(mesh):
    return jax.shard_map(
        shards,
        mesh=mesh,
        in_specs=(P(("src", "tgt"), None), P("tgt", None), P(("src", "tgt")), P("tgt"), P("tgt")),
        out_specs=(P(("src", "tgt")), P("tgt"), P(("src", "tgt"), None)),
        check_vma=False,
    )
```

time: 529 us -> 52.9 us (0.10)
  blocking collectives: 450 us -> 0 us
  Pallas kernels: 0 us -> 52 us
  waiting for transfers between devices: 42.4 us -> 0 us
  between operations: 14.8 us -> 0.64 us
  matrix products: 10.5 us -> 0 us
  other arithmetic: 8.08 us -> 0 us
    pmax x1 -> x0, blocking collectives: 146 us -> none  [shards(): whole_peak = lax.pmax(col_peak, 'src')]
    psum x1 -> x0, blocking collectives: 133 us -> none  [shards(): whole_total = lax.psum(col_total * jnp.exp(col_peak - whole_peak), 'src')]
    all_gather x3 -> x0, blocking collectives: 124 us -> none  [the longest x1 57.4 us: shards(): lax.all_gather(target_new, 'tgt', axis=0, tiled=True)]
    pallas_call x0 -> x2, Pallas kernels: none -> 52 us  [the longest x1 50.7 us: shards(): pl.pallas_call(kernel, name='sinkhorn', out_shape=shapes, in_specs=[hbm]...]
    unnamed x1 -> x0, blocking collectives: 47.5 us -> none
    all_gather x1 -> x0, waiting for transfers between devices: 41.7 us -> none  [shards(): lax.all_gather(points_tgt, 'tgt', axis=0, tiled=True)]
    dot_general x3 -> x0, matrix products: 10.5 us -> none  [the longest x2 6.77 us: pair_cost(): jnp.dot(rows_a, rows_b.T, precision=lax.Precision.HIGHEST, preferred_elem...]
    reduce_sum x7 -> x0, other arithmetic: 7.18 us -> none  [the longest x2 4.59 us: pair_cost(): right = 0.5 * jnp.sum(rows_b * rows_b, axis=1)]
  transfers between devices with their start and end apart: 1 -> 0, of which waited for: 1 -> 0; matrix products, arithmetic and copies ran while one was open for 1% -> 0% of each run, Pallas kernels for 0% -> 0%
where the time goes in v2:
time: 52.9 us; the launch traced here: 52.7 us
  Pallas kernels  52 us (98%)
  between operations  0.64 us (1%)
    pallas_call x1, Pallas kernels, shards(): pl.pallas_call(kernel, name='sinkhorn', out_shape=shapes, in_specs=[hbm]...  50.7 us
    pallas_call x1, Pallas kernels, shards(): pl.pallas_call(finish, name='finish', out_shape=shapes, in_specs=[vmem] *...  1.39 us

profile of v2, /device:TPU:1, one launch (start us, length us, event | category | flops | bytes accessed | tf_op | source)
XLA Modules:
  0.0 52.7 jit_solution(8410678710778354893)
XLA Ops:
  0.6 50.7 %sinkhorn.1 = (f32[1,64]{1,0:T(1,128)}, f32[4,128]{1,0:T(4,128)}, f32[64,128]{1,0:T(8,128)}) custom-call(f32[64,128]{1,0:T(8,128)} %ps.1, f32[512,128]{1,0:T(8,128)} %pt.1, f32[1,64]{1,0:T(1,128)} %bitcast.7, f32[4,128]{1,0:T(4,128)} %bitcast.5, f32[4,128]{1,0:T(4,128)} %bitcast.6), custom_call_target="tpu_custom_call" | custom-call | tf_op jit(solution)/shard_map/sinkhorn/pallas_call | solution.py:300
  51.3 1.4 %finish.1 = (f32[1,64]{1,0:T(1,128)}, f32[4,128]{1,0:T(4,128)}, f32[64,128]{1,0:T(8,128)}) custom-call(f32[1,64]{1,0:T(1,128)} %get-tuple-element.9.f_ref, f32[4,128]{1,0:T(4,128)} %get-tuple-element.10.t_ref, f32[64,128]{1,0:T(8,128)} %get-tuple-element.11.m_ref), custom_call_target="tpu_custom_call" | custom-call | tf_op jit(solution)/shard_map/finish/pallas_call | solution.py:348

commit v3 on v2

v3 whole, which is shorter than its diff:
```python
import jax
import jax.numpy as jnp
from jax import lax
from jax.experimental import pallas as pl
from jax.experimental.pallas import tpu as pltpu
from jax.sharding import PartitionSpec as P

MESH = pl.DeviceIdType.MESH
F32 = jnp.float32
BF16 = jnp.bfloat16
ROWS = 64
SLICE = 32
QUAD = 4 * ROWS


def ring(a):
    return min(a, 4 - a)


PEERS = sorted(((a, b) for a in range(4) for b in range(4) if a or b), key=lambda o: -ring(o[0]) - ring(o[1]))

GATHER_GROUPS = ((0, 1, 3, 2),)
MAP_GROUPS = ((2, 1, 3, 0),)


LOG2E = 1.4426950408889634
LN2 = 0.6931471805599453


def lse0(values):
    peak = jnp.max(values, axis=0, keepdims=True)
    return peak + LOG2E * jnp.log(jnp.sum(jnp.exp2(values - peak), axis=0, keepdims=True))


def split3(v):
    hi = v.astype(BF16)
    rest = v - hi.astype(F32)
    mid = rest.astype(BF16)
    return hi, mid, (rest - mid.astype(F32)).astype(BF16)


def kernel(
    ps, pt, ls, lt, gp,
    out_f, out_t, out_m,
    xs, tb, gv, lv, lsv, y1, y3, yf, yt, aa, ltb, sc, rb, uu, lsum, cl, cb, vv, mp, mm, mb, wt,
    loc, xs_s, xs_r, tb_s, tb_r, fw_r, rb_s, rb_r, cb_s, cb_r, mb_s, mb_r,
):
    s = lax.axis_index("src")
    t = lax.axis_index("tgt")
    q = s >> 1
    zl = t >> 1
    c = t & 1
    z = (s & 1) * 8 + zl
    x = q >> 2
    y = q & 3
    me = z * 2 + c

    def peer(a, b):
        return ((x + a) & 3) * 4 + ((y + b) & 3)

    def plane_device(p):
        return (p * 2 + (s & 1), t)

    def column_device(to_z, to_c):
        return (q * 2 + (to_z >> 3), (to_z & 7) * 2 + to_c)

    def remote(src, dst, send, recv, device):
        return pltpu.make_async_remote_copy(
            src_ref=src, dst_ref=dst, send_sem=send, recv_sem=recv, device_id=device, device_id_type=MESH
        )

    def take(ref, recv):
        remote(ref, ref, recv, recv, plane_device(peer(1, 0))).wait_recv()

    def left(ref, send):
        remote(ref, ref, send, send, plane_device(peer(1, 0))).wait_send()

    barrier = pltpu.get_barrier_semaphore()
    for d in (4, -4, 3, -3, 2, -2, 1, -1):
        for to_c in range(2):
            pl.semaphore_signal(
                barrier, inc=1, device_id=column_device((z + d) & 15, to_c), device_id_type=MESH
            )
    for a, b in PEERS:
        pl.semaphore_signal(barrier, inc=1, device_id=plane_device(peer(a, b)), device_id_type=MESH)
    pl.semaphore_signal(barrier, inc=1, device_id=column_device(z, 1 - c), device_id_type=MESH)

    local = [
        pltpu.make_async_copy(gp, gv, loc.at[0]),
        pltpu.make_async_copy(lt, lv, loc.at[1]),
        pltpu.make_async_copy(pt.at[pl.ds(pl.multiple_of(q * SLICE, SLICE), SLICE)], tb.at[t, pl.ds(0, SLICE)], loc.at[2]),
        pltpu.make_async_copy(ps, xs.at[q], loc.at[3]),
        pltpu.make_async_copy(ls, lsv, loc.at[4]),
    ]
    for copy in local:
        copy.start()
    for copy in local:
        copy.wait()
    tb[pl.ds(t, 1), SLICE : SLICE + 1] = gv[pl.ds(q >> 2, 1), :][None]
    tb[pl.ds(t, 1), SLICE + 1 : SLICE + 2] = lv[pl.ds(q >> 2, 1), :][None]

    pl.semaphore_wait(barrier, 16 + 15 + 1)

    def send_targets(slot, recv, device):
        remote(tb.at[slot], tb.at[slot], tb_s.at[0], recv, device).start()

    def send_points(a, b):
        remote(xs.at[q], xs.at[q], xs_s.at[0], xs_r.at[x], plane_device(peer(a, b))).start()

    sibling = column_device(z, 1 - c)
    send_targets(t, tb_r.at[3], column_device((z + 4 - 8 * c) & 15, c))
    for d, offsets in zip((3, -3, 2, -2, 1, -1), PEERS[0:6]):
        send_targets(t, tb_r.at[abs(d) - 1], column_device((z + d) & 15, c))
        send_points(*offsets)
    send_targets(t, fw_r.at[0], sibling)
    for offsets in PEERS[6:]:
        send_points(*offsets)

    lane = lax.broadcasted_iota(jnp.int32, (SLICE, 128), 1)
    sub = lax.broadcasted_iota(jnp.int32, (SLICE, 128), 0)
    mine = lane == sub + (q & 3) * SLICE

    def use_targets(slot):
        block = tb[pl.ds(slot, 1)][0]
        pts = block[0:SLICE]
        rows = pl.ds(pl.multiple_of(slot * SLICE, SLICE), SLICE)
        own = jnp.where(mine, 2.0 * block[SLICE : SLICE + 1], 0.0)
        a = LOG2E * jnp.sum(own - pts * pts, axis=1, keepdims=True)
        aa[rows, :] = jnp.broadcast_to(a, (SLICE, 128))
        hi, mid, lo = split3((2.0 * LOG2E) * pts)
        yf[rows, :] = pts
        y1[rows, 0:128] = hi
        y1[rows, 128:256] = mid
        y3[rows, 0:128] = hi
        y3[rows, 128:256] = lo

    def offsets_at(d):
        return (d, 8 - d) if d % 4 else (d,)

    def use_forwarded(d):
        take(tb.at[pl.ds(0, len(offsets_at(d)))], fw_r.at[d])
        for off in offsets_at(d):
            use_targets(((zl + off) & 7) * 2 + 1 - c)

    for d in (1, 2, 3, 4):
        take(tb.at[pl.ds(0, len(offsets_at(d)))], tb_r.at[d - 1])
        slots = [((zl + off) & 7) * 2 + c for off in offsets_at(d)]
        for slot in slots:
            send_targets(slot, fw_r.at[d], sibling)
        if d > 1:
            take(tb.at[pl.ds(0, len(offsets_at(d - 1)))], fw_r.at[d - 1])
    take(tb.at[0], fw_r.at[0])
    take(tb.at[0], fw_r.at[4])
    for slot in range(16):
        use_targets(slot)

    def product(targets, first, second):
        return lax.dot_general(
            targets, jnp.concatenate([first, second], axis=1),
            (((1,), (1,)), ((), ())), preferred_element_type=F32,
        )

    for group in GATHER_GROUPS:
        for a in group:
            take(xs.at[pl.ds(0, 4 if a else 3)], xs_r.at[(x + a) & 3])
        for a in group:
            quad = (x + a) & 3
            hi, mid, lo = split3(xs[pl.ds(quad * 4, 4)].reshape(QUAD, 128))
            prod = product(y3[...], lo, hi) + product(y1[...], mid, hi) + product(y1[...], hi, mid)
            score = prod + jnp.concatenate([aa[...], aa[...]], axis=1)
            sc[pl.ds(quad, 1)] = score[None]
            row = lse0(score)
            rb[pl.ds(q, 1), pl.ds(2 * quad, 1)] = row[:, 0:128][None]
            rb[pl.ds(q, 1), pl.ds(2 * quad + 1, 1)] = row[:, 128:256][None]

    half = (lax.broadcasted_iota(jnp.int32, (1, 128), 1) >> 6) == (q & 1)
    both = jnp.concatenate([lsv[...], lsv[...]], axis=1)
    rb[pl.ds(q, 1), 8:9] = jnp.where(half, both, 0.0)[None]
    for a, b in PEERS:
        remote(rb.at[q], rb.at[q], rb_s.at[0], rb_r.at[0], plane_device(peer(a, b))).start()

    for b in range(4):
        yb = yf[b * 128 : (b + 1) * 128, :].T
        hi = yb.astype(BF16)
        yt[0:128, b * 128 : (b + 1) * 128] = hi
        yt[128:256, b * 128 : (b + 1) * 128] = (yb - hi.astype(F32)).astype(BF16)
    for slot in range(16):
        l = LOG2E * jnp.sum(jnp.where(mine, tb[slot, SLICE + 1 : SLICE + 2], 0.0), axis=1, keepdims=True)
        ltb[slot * SLICE : (slot + 1) * SLICE, :] = jnp.broadcast_to(l, (SLICE, 128))
    own_points = xs[pl.ds(q, 1)][0]
    squares = jnp.concatenate([own_points * own_points, jnp.zeros((128 - ROWS, 128), F32)], axis=0)
    norm = jnp.sum(squares.T, axis=0, keepdims=True)

    take(rb.at[pl.ds(0, 15)], rb_r.at[0])
    rowlse = lse0(rb[:, 0:8])[0]
    uu[...] = rowlse
    for b in range(8):
        lsum[b : b + 1, :] = rb[2 * b, 8:9] + rb[2 * b + 1, 8:9]
    u = LOG2E * lsum[...] - rowlse

    def columns(j, carry):
        rows = pl.ds(pl.multiple_of(j * 32, 32), 32)
        vals = []
        for b in range(8):
            lanes = slice((b % 2) * 128, (b % 2) * 128 + 128)
            v = u[b : b + 1, :] + sc[b // 2, rows, lanes]
            sc[b // 2, rows, lanes] = v
            vals.append(v)
        peak = vals[0]
        for v in vals[1:]:
            peak = jnp.maximum(peak, v)
        total = jnp.exp2(vals[0] - peak)
        for v in vals[1:]:
            total = total + jnp.exp2(v - peak)
        cl[rows, :] = peak + LOG2E * jnp.log(total)
        return carry

    lax.fori_loop(0, 16, columns, 0, unroll=True)
    for b in range(4):
        cb[pl.ds(me, 1), b : b + 1] = lse0(cl[b * 128 : (b + 1) * 128, :].T)[None]

    def send_columns(d, to_c):
        remote(cb.at[me], cb.at[me], cb_s.at[0], cb_r.at[0], column_device((z + d) & 15, to_c)).start()

    for d in (8, 7, -7, 6, -6, 5, -5, 4, -4, 3, -3, 2, -2, 1, -1):
        for to_c in range(2):
            send_columns(d, to_c)
    send_columns(0, 1 - c)

    own_lse = uu[pl.ds(q >> 1, 1), :]
    own_lse = jnp.where(q & 1 == 0, own_lse, pltpu.roll(own_lse, 64, 1))
    out_f[...] = 0.5 * (lsv[...] + norm[:, 0:ROWS] - LN2 * own_lse[:, 0:ROWS])

    take(cb.at[pl.ds(0, 31)], cb_r.at[0])
    collse = lse0(cb[...])[0]
    for b in range(4):
        mp[b : b + 1, :] = collse[b : b + 1, :]
        spread = jnp.broadcast_to(collse[b : b + 1, :], (128, 128)).T
        vv[b * 128 : (b + 1) * 128, :] = ltb[b * 128 : (b + 1) * 128, :] - spread

    new_row = mp[pl.ds(t >> 2, 1), :]

    for group in MAP_GROUPS:
        for a in group:
            quad = (x + a) & 3
            w = jnp.exp2(sc[pl.ds(quad, 1)][0] + jnp.concatenate([vv[...], vv[...]], axis=1))
            total = jnp.sum(w, axis=0, keepdims=True)
            hi = w.astype(BF16)
            lo = (w - hi.astype(F32)).astype(BF16)
            first = jnp.dot(yt[...], hi, preferred_element_type=F32)
            second = jnp.dot(yt[0:128, :], lo, preferred_element_type=F32)
            n = first[0:128] + first[128:256] + second
            n = jnp.concatenate([n[:, 0:128].T, n[:, 128:256].T], axis=0)
            for h in range(4):
                lanes = slice((h // 2) * 128, (h // 2) * 128 + 128)
                part = jnp.concatenate([n[h * ROWS : (h + 1) * ROWS], total[:, lanes], new_row], axis=0)
                mm[pl.ds(quad * 4 + h, 1)] = part[None]
        for a in group:
            for b in (2, 1, 3, 0):
                if a or b:
                    p = peer(a, b)
                    remote(mm.at[p], mb.at[q], mb_s.at[0], mb_r.at[x], plane_device(p)).start()

    mb[pl.ds(q, 1)] = mm[pl.ds(q, 1)]
    total = jnp.zeros((ROWS + 1, 128), F32)
    for a in (0, 1, 3, 2):
        quad = (x + a) & 3
        take(mb.at[pl.ds(0, 4 if a else 3)], mb_r.at[quad])
        got = mb[pl.ds(quad * 4, 4), 0 : ROWS + 1]
        total = total + ((got[0] + got[1]) + (got[2] + got[3]))
    wt[...] = jnp.broadcast_to(1.0 / total[ROWS : ROWS + 1], (128, 128)).T
    out_m[...] = total[0:ROWS] * wt[pl.ds(pl.multiple_of((q & 1) * ROWS, ROWS), ROWS), :]

    pieces = mb[:, ROWS + 1 : ROWS + 2].reshape(16, 128)
    lane16 = lax.broadcasted_iota(jnp.int32, (16, 128), 1) >> 5
    sub16 = lax.broadcasted_iota(jnp.int32, (16, 128), 0) & 3
    whole = jnp.zeros((16, 128), F32)
    for k in range(4):
        turned = pltpu.roll(pieces, ((k - t) & 3) * SLICE, 1)
        whole = whole + jnp.where((lane16 == k) & (sub16 == k), turned, 0.0)
    for b in range(4):
        row = jnp.sum(whole[4 * b : 4 * b + 4], axis=0, keepdims=True)
        out_t[b : b + 1, :] = gv[b : b + 1, :] + 0.5 * (lv[b : b + 1, :] - LN2 * row)

    left(tb.at[pl.ds(0, 15)], tb_s.at[0])
    left(xs.at[pl.ds(0, 15)], xs_s.at[0])
    left(rb.at[pl.ds(0, 15)], rb_s.at[0])
    left(cb.at[pl.ds(0, 31)], cb_s.at[0])
    left(mm.at[pl.ds(0, 15)], mb_s.at[0])


def finish(f_ref, t_ref, m_ref, out_f, out_t, out_m):
    out_f[...] = f_ref[...]
    out_t[...] = t_ref[...]
    out_m[...] = m_ref[...]


def shards(points_src, points_tgt, log_source, log_target, target_potential):
    vmem = pl.BlockSpec(memory_space=pltpu.VMEM)
    hbm = pl.BlockSpec(memory_space=pltpu.HBM)
    dma = pltpu.SemaphoreType.DMA
    shapes = (
        jax.ShapeDtypeStruct((1, ROWS), F32),
        jax.ShapeDtypeStruct((4, 128), F32),
        jax.ShapeDtypeStruct((ROWS, 128), F32),
    )
    results = pl.pallas_call(
        kernel,
        name="sinkhorn",
        out_shape=shapes,
        in_specs=[hbm] * 5,
        out_specs=(vmem,) * 3,
        scratch_shapes=[
            pltpu.VMEM((16, ROWS, 128), F32),
            pltpu.VMEM((16, SLICE + 2, 128), F32),
            pltpu.VMEM((4, 128), F32),
            pltpu.VMEM((4, 128), F32),
            pltpu.VMEM((1, ROWS), F32),
            pltpu.VMEM((512, 256), BF16),
            pltpu.VMEM((512, 256), BF16),
            pltpu.VMEM((512, 128), F32),
            pltpu.VMEM((256, 512), BF16),
            pltpu.VMEM((512, 128), F32),
            pltpu.VMEM((512, 128), F32),
            pltpu.VMEM((4, 512, QUAD), F32),
            pltpu.VMEM((16, 9, 128), F32),
            pltpu.VMEM((8, 128), F32),
            pltpu.VMEM((8, 128), F32),
            pltpu.VMEM((512, 128), F32),
            pltpu.VMEM((32, 4, 128), F32),
            pltpu.VMEM((512, 128), F32),
            pltpu.VMEM((4, 128), F32),
            pltpu.VMEM((16, ROWS + 2, 128), F32),
            pltpu.VMEM((16, ROWS + 2, 128), F32),
            pltpu.VMEM((128, 128), F32),
            dma((5,)),
            dma((1,)), dma((4,)),
            dma((1,)), dma((4,)), dma((5,)),
            dma((1,)), dma((1,)),
            dma((1,)), dma((1,)),
            dma((1,)), dma((4,)),
        ],
        compiler_params=pltpu.CompilerParams(
            collective_id=0, has_side_effects=True, vmem_limit_bytes=56 * 2**20
        ),
    )(
        points_src,
        points_tgt,
        log_source.reshape(1, ROWS),
        log_target.reshape(4, 128),
        target_potential.reshape(4, 128),
    )
    source_potential, target_new, mapped = pl.pallas_call(
        finish, name="finish", out_shape=shapes, in_specs=[vmem] * 3, out_specs=(vmem,) * 3
    )(*results)
    return source_potential.reshape(ROWS), target_new.reshape(512), mapped


def solution(mesh):
    return jax.shard_map(
        shards,
        mesh=mesh,
        in_specs=(P(("src", "tgt"), None), P("tgt", None), P(("src", "tgt")), P("tgt"), P("tgt")),
        out_specs=(P(("src", "tgt")), P("tgt"), P(("src", "tgt"), None)),
        check_vma=False,
    )
```

time: 52.9 us -> 49.5 us (0.936)
  Pallas kernels: 52 us -> 48.6 us
    pallas_call x1, Pallas kernels: 50.7 us -> 47.2 us  [shards(): pl.pallas_call(kernel, name='sinkhorn', out_shape=shapes, in_specs=[hbm]...]
where the time goes in v3:
time: 49.5 us; the launch traced here: 49.3 us
  Pallas kernels  48.6 us (98%)
  between operations  0.64 us (1%)
    pallas_call x1, Pallas kernels, shards(): pl.pallas_call(kernel, name='sinkhorn', out_shape=shapes, in_specs=[hbm]...  47.2 us
    pallas_call x1, Pallas kernels, shards(): pl.pallas_call(finish, name='finish', out_shape=shapes, in_specs=[vmem] *...  1.39 us

profile of v3, /device:TPU:1, one launch (start us, length us, event | category | flops | bytes accessed | tf_op | source)
XLA Modules:
  0.0 49.3 jit_solution(13702923573489290623)
XLA Ops:
  0.6 47.2 %sinkhorn.1 = (f32[1,64]{1,0:T(1,128)}, f32[4,128]{1,0:T(4,128)}, f32[64,128]{1,0:T(8,128)}) custom-call(f32[64,128]{1,0:T(8,128)} %ps.1, f32[512,128]{1,0:T(8,128)} %pt.1, f32[1,64]{1,0:T(1,128)} %bitcast.7, f32[4,128]{1,0:T(4,128)} %bitcast.5, f32[4,128]{1,0:T(4,128)} %bitcast.6), custom_call_target="tpu_custom_call" | custom-call | tf_op jit(solution)/shard_map/sinkhorn/pallas_call | solution.py:307
  47.9 1.4 %finish.1 = (f32[1,64]{1,0:T(1,128)}, f32[4,128]{1,0:T(4,128)}, f32[64,128]{1,0:T(8,128)}) custom-call(f32[1,64]{1,0:T(1,128)} %get-tuple-element.9.f_ref, f32[4,128]{1,0:T(4,128)} %get-tuple-element.10.t_ref, f32[64,128]{1,0:T(8,128)} %get-tuple-element.11.m_ref), custom_call_target="tpu_custom_call" | custom-call | tf_op jit(solution)/shard_map/finish/pallas_call | solution.py:353

commit v4 on v3

--- a/solution.py
+++ b/solution.py
@@ -9,6 +9,7 @@
 F32 = jnp.float32
 BF16 = jnp.bfloat16
 ROWS = 64
+HALF = 32
 SLICE = 32
 QUAD = 4 * ROWS
 
@@ -18,10 +19,6 @@
 
 
 PEERS = sorted(((a, b) for a in range(4) for b in range(4) if a or b), key=lambda o: -ring(o[0]) - ring(o[1]))
-
-GATHER_GROUPS = ((0, 1, 3, 2),)
-MAP_GROUPS = ((2, 1, 3, 0),)
-
 
 LOG2E = 1.4426950408889634
 LN2 = 0.6931471805599453
@@ -39,10 +36,20 @@
     return hi, mid, (rest - mid.astype(F32)).astype(BF16)
 
 
+def gather_lanes(pieces, group):
+    lane = lax.broadcasted_iota(jnp.int32, (16, 128), 1) >> 5
+    row = lax.broadcasted_iota(jnp.int32, (16, 128), 0) & 3
+    whole = jnp.zeros((16, 128), F32)
+    for k in range(4):
+        turned = pltpu.roll(pieces, ((k - group) & 3) * SLICE, 1)
+        whole = whole + jnp.where((lane == k) & (row == k), turned, 0.0)
+    return jnp.concatenate([jnp.sum(whole[4 * b : 4 * b + 4], axis=0, keepdims=True) for b in range(4)], axis=0)
+
+
 def kernel(
     ps, pt, ls, lt, gp,
     out_f, out_t, out_m,
-    xs, tb, gv, lv, lsv, y1, y3, yf, yt, aa, ltb, sc, rb, uu, lsum, cl, cb, vv, mp, mm, mb, wt,
+    xs, tb, gv, lv, lsv, y1, y3, yf, yt, aa, sc, eh, el, fs, rb, uu, lsum, cl, cb, mp, mm, mb, wt,
     loc, xs_s, xs_r, tb_s, tb_r, fw_r, rb_s, rb_r, cb_s, cb_r, mb_s, mb_r,
 ):
     s = lax.axis_index("src")
@@ -104,17 +111,32 @@
     def send_targets(slot, recv, device):
         remote(tb.at[slot], tb.at[slot], tb_s.at[0], recv, device).start()
 
-    def send_points(a, b):
-        remote(xs.at[q], xs.at[q], xs_s.at[0], xs_r.at[x], plane_device(peer(a, b))).start()
+    def send_half(p, h, recv, to):
+        part = xs.at[p, pl.ds(h * HALF, HALF)]
+        remote(part, part, xs_s.at[0], recv, plane_device(to)).start()
+
+    def pass_on(p, h):
+        for k in (2, 1, 3):
+            send_half(p, h, xs_r.at[0], peer(k, 0) if h else peer(0, k))
 
     sibling = column_device(z, 1 - c)
     send_targets(t, tb_r.at[3], column_device((z + 4 - 8 * c) & 15, c))
-    for d, offsets in zip((3, -3, 2, -2, 1, -1), PEERS[0:6]):
+    for k in (2, 1, 3):
+        send_half(q, 0, xs_r.at[k], peer(k, 0))
+        send_half(q, 1, xs_r.at[3 + k], peer(0, k))
+    for d in (3, -3, 2, -2):
         send_targets(t, tb_r.at[abs(d) - 1], column_device((z + d) & 15, c))
-        send_points(*offsets)
+    pass_on(q, 0)
+    pass_on(q, 1)
+    for d in (1, -1):
+        send_targets(t, tb_r.at[abs(d) - 1], column_device((z + d) & 15, c))
     send_targets(t, fw_r.at[0], sibling)
-    for offsets in PEERS[6:]:
-        send_points(*offsets)
+    half_block = xs.at[0, pl.ds(0, HALF)]
+    for k in (1, 3, 2):
+        take(half_block, xs_r.at[k])
+        pass_on(peer(-k, 0), 0)
+        take(half_block, xs_r.at[3 + k])
+        pass_on(peer(0, -k), 1)
 
     lane = lax.broadcasted_iota(jnp.int32, (SLICE, 128), 1)
     sub = lax.broadcasted_iota(jnp.int32, (SLICE, 128), 0)
@@ -160,18 +182,15 @@
             (((1,), (1,)), ((), ())), preferred_element_type=F32,
         )
 
-    for group in GATHER_GROUPS:
-        for a in group:
-            take(xs.at[pl.ds(0, 4 if a else 3)], xs_r.at[(x + a) & 3])
-        for a in group:
-            quad = (x + a) & 3
-            hi, mid, lo = split3(xs[pl.ds(quad * 4, 4)].reshape(QUAD, 128))
-            prod = product(y3[...], lo, hi) + product(y1[...], mid, hi) + product(y1[...], hi, mid)
-            score = prod + jnp.concatenate([aa[...], aa[...]], axis=1)
-            sc[pl.ds(quad, 1)] = score[None]
-            row = lse0(score)
-            rb[pl.ds(q, 1), pl.ds(2 * quad, 1)] = row[:, 0:128][None]
-            rb[pl.ds(q, 1), pl.ds(2 * quad + 1, 1)] = row[:, 128:256][None]
+    take(xs.at[pl.ds(0, 12)], xs_r.at[0])
+    for quad in range(4):
+        hi, mid, lo = split3(xs[quad * 4 : quad * 4 + 4].reshape(QUAD, 128))
+        prod = product(y3[...], lo, hi) + product(y1[...], mid, hi) + product(y1[...], hi, mid)
+        score = prod + jnp.concatenate([aa[...], aa[...]], axis=1)
+        sc[quad] = score
+        row = lse0(score)
+        rb[pl.ds(q, 1), 2 * quad : 2 * quad + 1] = row[:, 0:128][None]
+        rb[pl.ds(q, 1), 2 * quad + 1 : 2 * quad + 2] = row[:, 128:256][None]
 
     half = (lax.broadcasted_iota(jnp.int32, (1, 128), 1) >> 6) == (q & 1)
     both = jnp.concatenate([lsv[...], lsv[...]], axis=1)
@@ -180,13 +199,8 @@
         remote(rb.at[q], rb.at[q], rb_s.at[0], rb_r.at[0], plane_device(peer(a, b))).start()
 
     for b in range(4):
-        yb = yf[b * 128 : (b + 1) * 128, :].T
-        hi = yb.astype(BF16)
-        yt[0:128, b * 128 : (b + 1) * 128] = hi
-        yt[128:256, b * 128 : (b + 1) * 128] = (yb - hi.astype(F32)).astype(BF16)
-    for slot in range(16):
-        l = LOG2E * jnp.sum(jnp.where(mine, tb[slot, SLICE + 1 : SLICE + 2], 0.0), axis=1, keepdims=True)
-        ltb[slot * SLICE : (slot + 1) * SLICE, :] = jnp.broadcast_to(l, (SLICE, 128))
+        yt[:, b * 128 : (b + 1) * 128] = yf[b * 128 : (b + 1) * 128, :].T
+    log_target = LOG2E * gather_lanes(tb[:, SLICE + 1 : SLICE + 2].reshape(16, 128), q & 3)
     own_points = xs[pl.ds(q, 1)][0]
     squares = jnp.concatenate([own_points * own_points, jnp.zeros((128 - ROWS, 128), F32)], axis=0)
     norm = jnp.sum(squares.T, axis=0, keepdims=True)
@@ -216,8 +230,11 @@
         return carry
 
     lax.fori_loop(0, 16, columns, 0, unroll=True)
+    tops = []
     for b in range(4):
-        cb[pl.ds(me, 1), b : b + 1] = lse0(cl[b * 128 : (b + 1) * 128, :].T)[None]
+        turned = cl[b * 128 : (b + 1) * 128, :].T
+        tops.append(jnp.max(turned, axis=0, keepdims=True))
+        cb[pl.ds(me, 1), b : b + 1] = lse0(turned)[None]
 
     def send_columns(d, to_c):
         remote(cb.at[me], cb.at[me], cb_s.at[0], cb_r.at[0], column_device((z + d) & 15, to_c)).start()
@@ -231,35 +248,50 @@
     own_lse = jnp.where(q & 1 == 0, own_lse, pltpu.roll(own_lse, 64, 1))
     out_f[...] = 0.5 * (lsv[...] + norm[:, 0:ROWS] - LN2 * own_lse[:, 0:ROWS])
 
+    def weights(j, carry):
+        rows = pl.ds(pl.multiple_of(j * 32, 32), 32)
+        top = jnp.max(cl[rows, :], axis=1, keepdims=True)
+        for quad in range(4):
+            w = jnp.exp2(sc[quad, rows, :] - top)
+            hi = w.astype(BF16)
+            eh[quad, rows, :] = hi
+            el[quad, rows, :] = (w - hi.astype(F32)).astype(BF16)
+        return carry
+
+    lax.fori_loop(0, 16, weights, 0)
+
     take(cb.at[pl.ds(0, 31)], cb_r.at[0])
     collse = lse0(cb[...])[0]
+    mp[...] = collse
+    new_row = mp[pl.ds(t >> 2, 1), :]
+    factor = jnp.exp2(log_target + jnp.concatenate(tops, axis=0) - collse)
+    lead = lax.broadcasted_iota(jnp.int32, (16, 128), 0)
     for b in range(4):
-        mp[b : b + 1, :] = collse[b : b + 1, :]
-        spread = jnp.broadcast_to(collse[b : b + 1, :], (128, 128)).T
-        vv[b * 128 : (b + 1) * 128, :] = ltb[b * 128 : (b + 1) * 128, :] - spread
-
-    new_row = mp[pl.ds(t >> 2, 1), :]
-
-    for group in MAP_GROUPS:
-        for a in group:
-            quad = (x + a) & 3
-            w = jnp.exp2(sc[pl.ds(quad, 1)][0] + jnp.concatenate([vv[...], vv[...]], axis=1))
-            total = jnp.sum(w, axis=0, keepdims=True)
-            hi = w.astype(BF16)
-            lo = (w - hi.astype(F32)).astype(BF16)
-            first = jnp.dot(yt[...], hi, preferred_element_type=F32)
-            second = jnp.dot(yt[0:128, :], lo, preferred_element_type=F32)
-            n = first[0:128] + first[128:256] + second
-            n = jnp.concatenate([n[:, 0:128].T, n[:, 128:256].T], axis=0)
-            for h in range(4):
-                lanes = slice((h // 2) * 128, (h // 2) * 128 + 128)
-                part = jnp.concatenate([n[h * ROWS : (h + 1) * ROWS], total[:, lanes], new_row], axis=0)
-                mm[pl.ds(quad * 4 + h, 1)] = part[None]
-        for a in group:
-            for b in (2, 1, 3, 0):
-                if a or b:
-                    p = peer(a, b)
-                    remote(mm.at[p], mb.at[q], mb_s.at[0], mb_r.at[x], plane_device(p)).start()
+        lanes = slice(b * 128, (b + 1) * 128)
+        f = factor[b : b + 1, :]
+        scaled = yt[:, lanes] * f
+        hi = scaled.astype(BF16)
+        fs[0:128, lanes] = hi
+        fs[144:272, lanes] = (scaled - hi.astype(F32)).astype(BF16)
+        top = f.astype(BF16).astype(F32)
+        fs[128:144, lanes] = jnp.where(lead == 0, top, jnp.where(lead == 1, f - top, 0.0)).astype(BF16)
+
+    for a in (2, 1, 3, 0):
+        quad = (x + a) & 3
+        first = jnp.dot(fs[...], eh[pl.ds(quad, 1)][0], preferred_element_type=F32)
+        second = jnp.dot(fs[0:144, :], el[pl.ds(quad, 1)][0], preferred_element_type=F32)
+        n = first[0:128] + first[144:272] + second[0:128]
+        total = first[128:129] + first[129:130] + second[128:129]
+        n = jnp.concatenate([n[:, 0:128].T, n[:, 128:256].T], axis=0)
+        for h in range(4):
+            lanes = slice((h // 2) * 128, (h // 2) * 128 + 128)
+            part = jnp.concatenate([n[h * ROWS : (h + 1) * ROWS], total[:, lanes], new_row], axis=0)
+            mm[pl.ds(quad * 4 + h, 1)] = part[None]
+    for a in (2, 1, 3, 0):
+        for b in (2, 1, 3, 0):
+            if a or b:
+                p = peer(a, b)
+                remote(mm.at[p], mb.at[q], mb_s.at[0], mb_r.at[x], plane_device(p)).start()
 
     mb[pl.ds(q, 1)] = mm[pl.ds(q, 1)]
     total = jnp.zeros((ROWS + 1, 128), F32)
@@ -271,16 +303,8 @@
     wt[...] = jnp.broadcast_to(1.0 / total[ROWS : ROWS + 1], (128, 128)).T
     out_m[...] = total[0:ROWS] * wt[pl.ds(pl.multiple_of((q & 1) * ROWS, ROWS), ROWS), :]
 
-    pieces = mb[:, ROWS + 1 : ROWS + 2].reshape(16, 128)
-    lane16 = lax.broadcasted_iota(jnp.int32, (16, 128), 1) >> 5
-    sub16 = lax.broadcasted_iota(jnp.int32, (16, 128), 0) & 3
-    whole = jnp.zeros((16, 128), F32)
-    for k in range(4):
-        turned = pltpu.roll(pieces, ((k - t) & 3) * SLICE, 1)
-        whole = whole + jnp.where((lane16 == k) & (sub16 == k), turned, 0.0)
-    for b in range(4):
-        row = jnp.sum(whole[4 * b : 4 * b + 4], axis=0, keepdims=True)
-        out_t[b : b + 1, :] = gv[b : b + 1, :] + 0.5 * (lv[b : b + 1, :] - LN2 * row)
+    new = gather_lanes(mb[:, ROWS + 1 : ROWS + 2].reshape(16, 128), t & 3)
+    out_t[...] = gv[...] + 0.5 * (lv[...] - LN2 * new)
 
     left(tb.at[pl.ds(0, 15)], tb_s.at[0])
     left(xs.at[pl.ds(0, 15)], xs_s.at[0])
@@ -319,22 +343,23 @@
             pltpu.VMEM((512, 256), BF16),
             pltpu.VMEM((512, 256), BF16),
             pltpu.VMEM((512, 128), F32),
-            pltpu.VMEM((256, 512), BF16),
-            pltpu.VMEM((512, 128), F32),
+            pltpu.VMEM((128, 512), F32),
             pltpu.VMEM((512, 128), F32),
             pltpu.VMEM((4, 512, QUAD), F32),
+            pltpu.VMEM((4, 512, QUAD), BF16),
+            pltpu.VMEM((4, 512, QUAD), BF16),
+            pltpu.VMEM((272, 512), BF16),
             pltpu.VMEM((16, 9, 128), F32),
             pltpu.VMEM((8, 128), F32),
             pltpu.VMEM((8, 128), F32),
             pltpu.VMEM((512, 128), F32),
             pltpu.VMEM((32, 4, 128), F32),
-            pltpu.VMEM((512, 128), F32),
             pltpu.VMEM((4, 128), F32),
             pltpu.VMEM((16, ROWS + 2, 128), F32),
             pltpu.VMEM((16, ROWS + 2, 128), F32),
             pltpu.VMEM((128, 128), F32),
             dma((5,)),
-            dma((1,)), dma((4,)),
+            dma((1,)), dma((7,)),
             dma((1,)), dma((4,)), dma((5,)),
             dma((1,)), dma((1,)),
             dma((1,)), dma((1,)),

time: 49.5 us -> 49.2 us (level)
  no operation moved by 1% of the time
where the time goes in v4:
time: 49.2 us; the launch traced here: 48.9 us
  Pallas kernels  48.3 us (98%)
  between operations  0.64 us (1%)
    pallas_call x1, Pallas kernels, shards(): pl.pallas_call(kernel, name='sinkhorn', out_shape=shapes, in_specs=[hbm]...  46.9 us
    pallas_call x1, Pallas kernels, shards(): pl.pallas_call(finish, name='finish', out_shape=shapes, in_specs=[vmem] *...  1.39 us

profile of v4, /device:TPU:1, one launch (start us, length us, event | category | flops | bytes accessed | tf_op | source)
XLA Modules:
  0.0 48.9 jit_solution(7635338923326748296)
XLA Ops:
  0.6 46.9 %sinkhorn.1 = (f32[1,64]{1,0:T(1,128)}, f32[4,128]{1,0:T(4,128)}, f32[64,128]{1,0:T(8,128)}) custom-call(f32[64,128]{1,0:T(8,128)} %ps.1, f32[512,128]{1,0:T(8,128)} %pt.1, f32[1,64]{1,0:T(1,128)} %bitcast.7, f32[4,128]{1,0:T(4,128)} %bitcast.5, f32[4,128]{1,0:T(4,128)} %bitcast.6), custom_call_target="tpu_custom_call" | custom-call | tf_op jit(solution)/shard_map/sinkhorn/pallas_call | solution.py:331
  47.6 1.4 %finish.1 = (f32[1,64]{1,0:T(1,128)}, f32[4,128]{1,0:T(4,128)}, f32[64,128]{1,0:T(8,128)}) custom-call(f32[1,64]{1,0:T(1,128)} %get-tuple-element.9.f_ref, f32[4,128]{1,0:T(4,128)} %get-tuple-element.10.t_ref, f32[64,128]{1,0:T(8,128)} %get-tuple-element.11.m_ref), custom_call_target="tpu_custom_call" | custom-call | tf_op jit(solution)/shard_map/finish/pallas_call | solution.py:378

commit v5 on v4

--- a/solution.py
+++ b/solution.py
@@ -50,7 +50,7 @@
     ps, pt, ls, lt, gp,
     out_f, out_t, out_m,
     xs, tb, gv, lv, lsv, y1, y3, yf, yt, aa, sc, eh, el, fs, rb, uu, lsum, cl, cb, mp, mm, mb, wt,
-    loc, xs_s, xs_r, tb_s, tb_r, fw_r, rb_s, rb_r, cb_s, cb_r, mb_s, mb_r,
+    known, loc, xs_s, xs_r, tb_s, tb_r, fw_r, rb_s, rb_r, cb_s, cb_r, mb_s, mb_r,
 ):
     s = lax.axis_index("src")
     t = lax.axis_index("tgt")
@@ -83,14 +83,17 @@
         remote(ref, ref, send, send, plane_device(peer(1, 0))).wait_send()
 
     barrier = pltpu.get_barrier_semaphore()
-    for d in (4, -4, 3, -3, 2, -2, 1, -1):
-        for to_c in range(2):
-            pl.semaphore_signal(
-                barrier, inc=1, device_id=column_device((z + d) & 15, to_c), device_id_type=MESH
-            )
-    for a, b in PEERS:
-        pl.semaphore_signal(barrier, inc=1, device_id=plane_device(peer(a, b)), device_id_type=MESH)
-    pl.semaphore_signal(barrier, inc=1, device_id=column_device(z, 1 - c), device_id_type=MESH)
+
+    def greet(device, sem=barrier):
+        pl.semaphore_signal(sem, inc=1, device_id=device, device_id_type=MESH)
+
+    sibling = column_device(z, 1 - c)
+    for k in (2, 1, 3):
+        greet(plane_device(peer(k, 0)))
+        greet(plane_device(peer(0, k)))
+    for d in (2, -2, 1, -1):
+        greet(column_device((z + d) & 15, c))
+    greet(sibling)
 
     local = [
         pltpu.make_async_copy(gp, gv, loc.at[0]),
@@ -106,7 +109,7 @@
     tb[pl.ds(t, 1), SLICE : SLICE + 1] = gv[pl.ds(q >> 2, 1), :][None]
     tb[pl.ds(t, 1), SLICE + 1 : SLICE + 2] = lv[pl.ds(q >> 2, 1), :][None]
 
-    pl.semaphore_wait(barrier, 16 + 15 + 1)
+    pl.semaphore_wait(barrier, 6 + 4 + 1)
 
     def send_targets(slot, recv, device):
         remote(tb.at[slot], tb.at[slot], tb_s.at[0], recv, device).start()
@@ -119,24 +122,42 @@
         for k in (2, 1, 3):
             send_half(p, h, xs_r.at[0], peer(k, 0) if h else peer(0, k))
 
-    sibling = column_device(z, 1 - c)
-    send_targets(t, tb_r.at[3], column_device((z + 4 - 8 * c) & 15, c))
+    def column_slot(off, core):
+        return ((zl + off) & 7) * 2 + core
+
     for k in (2, 1, 3):
         send_half(q, 0, xs_r.at[k], peer(k, 0))
         send_half(q, 1, xs_r.at[3 + k], peer(0, k))
-    for d in (3, -3, 2, -2):
-        send_targets(t, tb_r.at[abs(d) - 1], column_device((z + d) & 15, c))
+    send_targets(t, tb_r.at[1], column_device((z + 2) & 15, c))
+    send_targets(t, tb_r.at[2], column_device((z - 2) & 15, c))
     pass_on(q, 0)
     pass_on(q, 1)
     for d in (1, -1):
-        send_targets(t, tb_r.at[abs(d) - 1], column_device((z + d) & 15, c))
+        send_targets(t, tb_r.at[0], column_device((z + d) & 15, c))
     send_targets(t, fw_r.at[0], sibling)
     half_block = xs.at[0, pl.ds(0, HALF)]
-    for k in (1, 3, 2):
+
+    def relay_points(k):
         take(half_block, xs_r.at[k])
         pass_on(peer(-k, 0), 0)
         take(half_block, xs_r.at[3 + k])
         pass_on(peer(0, -k), 1)
+
+    relay_points(1)
+    take(tb.at[pl.ds(0, 2)], tb_r.at[0])
+    take(tb.at[0], tb_r.at[1])
+    take(tb.at[0], tb_r.at[2])
+    turn = 2 - 4 * c
+    for core in range(2):
+        send_targets(column_slot(-turn, c), tb_r.at[4], column_device((z + turn) & 15, core))
+    for sign in (1, -1):
+        for core in range(2):
+            send_targets(column_slot(-2 * sign, c), tb_r.at[3], column_device((z + sign) & 15, core))
+    relay_points(3)
+    relay_points(2)
+    for d in (1, 2):
+        for off in (d, 8 - d):
+            send_targets(column_slot(off, c), fw_r.at[d], sibling)
 
     lane = lax.broadcasted_iota(jnp.int32, (SLICE, 128), 1)
     sub = lax.broadcasted_iota(jnp.int32, (SLICE, 128), 0)
@@ -156,25 +177,21 @@
         y3[rows, 0:128] = hi
         y3[rows, 128:256] = lo
 
-    def offsets_at(d):
-        return (d, 8 - d) if d % 4 else (d,)
-
-    def use_forwarded(d):
-        take(tb.at[pl.ds(0, len(offsets_at(d)))], fw_r.at[d])
-        for off in offsets_at(d):
-            use_targets(((zl + off) & 7) * 2 + 1 - c)
-
-    for d in (1, 2, 3, 4):
-        take(tb.at[pl.ds(0, len(offsets_at(d)))], tb_r.at[d - 1])
-        slots = [((zl + off) & 7) * 2 + c for off in offsets_at(d)]
-        for slot in slots:
-            send_targets(slot, fw_r.at[d], sibling)
-        if d > 1:
-            take(tb.at[pl.ds(0, len(offsets_at(d - 1)))], fw_r.at[d - 1])
-    take(tb.at[0], fw_r.at[0])
-    take(tb.at[0], fw_r.at[4])
-    for slot in range(16):
-        use_targets(slot)
+    groups = (
+        (fw_r.at[0], 1, (0,)),
+        (fw_r.at[1], 2, (1, 7)),
+        (fw_r.at[2], 2, (2, 6)),
+        (tb_r.at[4], 2, (4,)),
+        (tb_r.at[3], 4, (3, 5)),
+    )
+    for sem, count, offsets in groups:
+        take(tb.at[pl.ds(0, count)], sem)
+        for off in offsets:
+            for core in range(2):
+                use_targets(column_slot(off, core))
+    for d in (2, -2):
+        for core in range(2):
+            greet(column_device((z + d) & 15, core), known)
 
     def product(targets, first, second):
         return lax.dot_general(
@@ -236,6 +253,8 @@
         tops.append(jnp.max(turned, axis=0, keepdims=True))
         cb[pl.ds(me, 1), b : b + 1] = lse0(turned)[None]
 
+    pl.semaphore_wait(known, 4)
+
     def send_columns(d, to_c):
         remote(cb.at[me], cb.at[me], cb_s.at[0], cb_r.at[0], column_device((z + d) & 15, to_c)).start()
 
@@ -331,7 +350,7 @@
     results = pl.pallas_call(
         kernel,
         name="sinkhorn",
-        out_shape=shapes,
+        out_shape=tuple(pltpu.VMEM(v.shape, v.dtype) for v in shapes),
         in_specs=[hbm] * 5,
         out_specs=(vmem,) * 3,
         scratch_shapes=[
@@ -358,26 +377,32 @@
             pltpu.VMEM((16, ROWS + 2, 128), F32),
             pltpu.VMEM((16, ROWS + 2, 128), F32),
             pltpu.VMEM((128, 128), F32),
+            pltpu.SemaphoreType.REGULAR,
             dma((5,)),
             dma((1,)), dma((7,)),
-            dma((1,)), dma((4,)), dma((5,)),
+            dma((1,)), dma((5,)), dma((3,)),
             dma((1,)), dma((1,)),
             dma((1,)), dma((1,)),
             dma((1,)), dma((4,)),
         ],
         compiler_params=pltpu.CompilerParams(
-            collective_id=0, has_side_effects=True, vmem_limit_bytes=56 * 2**20
+            collective_id=0, has_side_effects=True, vmem_limit_bytes=40 * 2**20
         ),
     )(
-        points_src,
-        points_tgt,
-        log_source.reshape(1, ROWS),
-        log_target.reshape(4, 128),
-        target_potential.reshape(4, 128),
+        *(
+            pltpu.with_memory_space_constraint(v, pltpu.HBM)
+            for v in (
+                points_src,
+                points_tgt,
+                log_source.reshape(1, ROWS),
+                log_target.reshape(4, 128),
+                target_potential.reshape(4, 128),
+            )
+        )
     )
     source_potential, target_new, mapped = pl.pallas_call(
         finish, name="finish", out_shape=shapes, in_specs=[vmem] * 3, out_specs=(vmem,) * 3
-    )(*results)
+    )(*(pltpu.with_memory_space_constraint(v, pltpu.VMEM) for v in results))
     return source_potential.reshape(ROWS), target_new.reshape(512), mapped
 
 

time: 49.2 us -> 46.9 us (0.953)
  Pallas kernels: 48.3 us -> 46 us
    pallas_call x1, Pallas kernels: 46.9 us -> 45.4 us  [shards(): pl.pallas_call(kernel, name='sinkhorn', out_shape=tuple((pltpu.VMEM(v.sha...]
    pallas_call x1, Pallas kernels: 1.39 us -> 0.63 us  [shards(): pl.pallas_call(finish, name='finish', out_shape=shapes, in_specs=[vmem] *...]
where the time goes in v5:
time: 46.9 us; the launch traced here: 46.7 us
  Pallas kernels  46 us (98%)
  between operations  0.64 us (1%)
    pallas_call x1, Pallas kernels, shards(): pl.pallas_call(kernel, name='sinkhorn', out_shape=tuple((pltpu.VMEM(v.sha...  45.4 us

profile of v5, /device:TPU:1, one launch (start us, length us, event | category | flops | bytes accessed | tf_op | source)
XLA Modules:
  0.0 46.7 jit_solution(6036574192585518092)
XLA Ops:
  0.6 45.4 %sinkhorn.1 = (f32[1,64]{1,0:T(1,128)S(1)}, f32[4,128]{1,0:T(4,128)S(1)}, f32[64,128]{1,0:T(8,128)S(1)}) custom-call(f32[64,128]{1,0:T(8,128)} %ps.1, f32[512,128]{1,0:T(8,128)} %pt.1, f32[1,64]{1,0:T(1,128)} %bitcast.7, f32[4,128]{1,0:T(4,128)} %bitcast.5, f32[4,128]{1,0:T(4,128)} %bitcast.6), custom_call_target="tpu_custom_call" | custom-call | tf_op jit(solution)/shard_map/sinkhorn/pallas_call | solution.py:350
  46.0 0.6 %finish.1 = (f32[1,64]{1,0:T(1,128)}, f32[4,128]{1,0:T(4,128)}, f32[64,128]{1,0:T(8,128)}) custom-call(f32[1,64]{1,0:T(1,128)S(1)} %get-tuple-element.9.f_ref, f32[4,128]{1,0:T(4,128)S(1)} %get-tuple-element.10.t_ref, f32[64,128]{1,0:T(8,128)S(1)} %get-tuple-element.11.m_ref), custom_call_target="tpu_custom_call" | custom-call | tf_op jit(solution)/shard_map/finish/pallas_call | solution.py:403

commit v6 on v5

--- a/solution.py
+++ b/solution.py
@@ -125,15 +125,15 @@
     def column_slot(off, core):
         return ((zl + off) & 7) * 2 + core
 
-    for k in (2, 1, 3):
+    send_targets(t, tb_r.at[1], column_device((z + 2) & 15, c))
+    send_targets(t, tb_r.at[2], column_device((z - 2) & 15, c))
+    for k in (1, 3, 2):
         send_half(q, 0, xs_r.at[k], peer(k, 0))
         send_half(q, 1, xs_r.at[3 + k], peer(0, k))
-    send_targets(t, tb_r.at[1], column_device((z + 2) & 15, c))
-    send_targets(t, tb_r.at[2], column_device((z - 2) & 15, c))
+    for d in (1, -1):
+        send_targets(t, tb_r.at[0], column_device((z + d) & 15, c))
     pass_on(q, 0)
     pass_on(q, 1)
-    for d in (1, -1):
-        send_targets(t, tb_r.at[0], column_device((z + d) & 15, c))
     send_targets(t, fw_r.at[0], sibling)
     half_block = xs.at[0, pl.ds(0, HALF)]
 
@@ -314,9 +314,9 @@
 
     mb[pl.ds(q, 1)] = mm[pl.ds(q, 1)]
     total = jnp.zeros((ROWS + 1, 128), F32)
-    for a in (0, 1, 3, 2):
-        quad = (x + a) & 3
-        take(mb.at[pl.ds(0, 4 if a else 3)], mb_r.at[quad])
+    for a in range(4):
+        take(mb.at[pl.ds(0, 4 if a else 3)], mb_r.at[(x + a) & 3])
+    for quad in range(4):
         got = mb[pl.ds(quad * 4, 4), 0 : ROWS + 1]
         total = total + ((got[0] + got[1]) + (got[2] + got[3]))
     wt[...] = jnp.broadcast_to(1.0 / total[ROWS : ROWS + 1], (128, 128)).T

time: 46.9 us -> 46.8 us (level)
  no operation moved by 1% of the time
where the time goes in v6:
time: 46.8 us; the launch traced here: 46.7 us
  Pallas kernels  46 us (98%)
  between operations  0.64 us (1%)
    pallas_call x1, Pallas kernels, shards(): pl.pallas_call(kernel, name='sinkhorn', out_shape=tuple((pltpu.VMEM(v.sha...  45.4 us

profile of v6, /device:TPU:1, one launch (start us, length us, event | category | flops | bytes accessed | tf_op | source)
XLA Modules:
  0.0 46.7 jit_solution(11243832360903163642)
XLA Ops:
  0.6 45.4 %sinkhorn.1 = (f32[1,64]{1,0:T(1,128)S(1)}, f32[4,128]{1,0:T(4,128)S(1)}, f32[64,128]{1,0:T(8,128)S(1)}) custom-call(f32[64,128]{1,0:T(8,128)} %ps.1, f32[512,128]{1,0:T(8,128)} %pt.1, f32[1,64]{1,0:T(1,128)} %bitcast.7, f32[4,128]{1,0:T(4,128)} %bitcast.5, f32[4,128]{1,0:T(4,128)} %bitcast.6), custom_call_target="tpu_custom_call" | custom-call | tf_op jit(solution)/shard_map/sinkhorn/pallas_call | solution.py:350
  46.0 0.6 %finish.1 = (f32[1,64]{1,0:T(1,128)}, f32[4,128]{1,0:T(4,128)}, f32[64,128]{1,0:T(8,128)}) custom-call(f32[1,64]{1,0:T(1,128)S(1)} %get-tuple-element.9.f_ref, f32[4,128]{1,0:T(4,128)S(1)} %get-tuple-element.10.t_ref, f32[64,128]{1,0:T(8,128)S(1)} %get-tuple-element.11.m_ref), custom_call_target="tpu_custom_call" | custom-call | tf_op jit(solution)/shard_map/finish/pallas_call | solution.py:403

commit v7 on v6

--- a/solution.py
+++ b/solution.py
@@ -104,7 +104,7 @@
     ]
     for copy in local:
         copy.start()
-    for copy in local:
+    for copy in local[:3]:
         copy.wait()
     tb[pl.ds(t, 1), SLICE : SLICE + 1] = gv[pl.ds(q >> 2, 1), :][None]
     tb[pl.ds(t, 1), SLICE + 1 : SLICE + 2] = lv[pl.ds(q >> 2, 1), :][None]
@@ -114,13 +114,14 @@
     def send_targets(slot, recv, device):
         remote(tb.at[slot], tb.at[slot], tb_s.at[0], recv, device).start()
 
-    def send_half(p, h, recv, to):
-        part = xs.at[p, pl.ds(h * HALF, HALF)]
-        remote(part, part, xs_s.at[0], recv, plane_device(to)).start()
-
-    def pass_on(p, h):
+    def send_half(p, h, recv, to, own=False):
+        rows = pl.ds(h * HALF, HALF)
+        part = xs.at[p, rows]
+        remote(ps.at[rows] if own else part, part, xs_s.at[0], recv, plane_device(to)).start()
+
+    def pass_on(p, h, own=False):
         for k in (2, 1, 3):
-            send_half(p, h, xs_r.at[0], peer(k, 0) if h else peer(0, k))
+            send_half(p, h, xs_r.at[0], peer(k, 0) if h else peer(0, k), own)
 
     def column_slot(off, core):
         return ((zl + off) & 7) * 2 + core
@@ -128,12 +129,12 @@
     send_targets(t, tb_r.at[1], column_device((z + 2) & 15, c))
     send_targets(t, tb_r.at[2], column_device((z - 2) & 15, c))
     for k in (1, 3, 2):
-        send_half(q, 0, xs_r.at[k], peer(k, 0))
-        send_half(q, 1, xs_r.at[3 + k], peer(0, k))
+        send_half(q, 0, xs_r.at[k], peer(k, 0), True)
+        send_half(q, 1, xs_r.at[3 + k], peer(0, k), True)
     for d in (1, -1):
         send_targets(t, tb_r.at[0], column_device((z + d) & 15, c))
-    pass_on(q, 0)
-    pass_on(q, 1)
+    pass_on(q, 0, True)
+    pass_on(q, 1, True)
     send_targets(t, fw_r.at[0], sibling)
     half_block = xs.at[0, pl.ds(0, HALF)]
 
@@ -199,6 +200,8 @@
             (((1,), (1,)), ((), ())), preferred_element_type=F32,
         )
 
+    for copy in local[3:]:
+        copy.wait()
     take(xs.at[pl.ds(0, 12)], xs_r.at[0])
     for quad in range(4):
         hi, mid, lo = split3(xs[quad * 4 : quad * 4 + 4].reshape(QUAD, 128))

time: 46.8 us -> 46.8 us (level)
  no operation moved by 1% of the time
where the time goes in v7:
time: 46.8 us; the launch traced here: 46.7 us
  Pallas kernels  46 us (98%)
  between operations  0.64 us (1%)
    pallas_call x1, Pallas kernels, shards(): pl.pallas_call(kernel, name='sinkhorn', out_shape=tuple((pltpu.VMEM(v.sha...  45.4 us

profile of v7, /device:TPU:1, one launch (start us, length us, event | category | flops | bytes accessed | tf_op | source)
XLA Modules:
  0.0 46.7 jit_solution(2919153685028126742)
XLA Ops:
  0.6 45.4 %sinkhorn.1 = (f32[1,64]{1,0:T(1,128)S(1)}, f32[4,128]{1,0:T(4,128)S(1)}, f32[64,128]{1,0:T(8,128)S(1)}) custom-call(f32[64,128]{1,0:T(8,128)} %ps.1, f32[512,128]{1,0:T(8,128)} %pt.1, f32[1,64]{1,0:T(1,128)} %bitcast.7, f32[4,128]{1,0:T(4,128)} %bitcast.5, f32[4,128]{1,0:T(4,128)} %bitcast.6), custom_call_target="tpu_custom_call" | custom-call | tf_op jit(solution)/shard_map/sinkhorn/pallas_call | solution.py:353
  46.0 0.6 %finish.1 = (f32[1,64]{1,0:T(1,128)}, f32[4,128]{1,0:T(4,128)}, f32[64,128]{1,0:T(8,128)}) custom-call(f32[1,64]{1,0:T(1,128)S(1)} %get-tuple-element.9.f_ref, f32[4,128]{1,0:T(4,128)S(1)} %get-tuple-element.10.t_ref, f32[64,128]{1,0:T(8,128)S(1)} %get-tuple-element.11.m_ref), custom_call_target="tpu_custom_call" | custom-call | tf_op jit(solution)/shard_map/finish/pallas_call | solution.py:406

commit v8 on v6

--- a/solution.py
+++ b/solution.py
@@ -310,12 +310,11 @@
         for b in (2, 1, 3, 0):
             if a or b:
                 p = peer(a, b)
-                remote(mm.at[p], mb.at[q], mb_s.at[0], mb_r.at[x], plane_device(p)).start()
+                remote(mm.at[p], mb.at[q], mb_s.at[0], mb_r.at[0], plane_device(p)).start()
 
     mb[pl.ds(q, 1)] = mm[pl.ds(q, 1)]
     total = jnp.zeros((ROWS + 1, 128), F32)
-    for a in range(4):
-        take(mb.at[pl.ds(0, 4 if a else 3)], mb_r.at[(x + a) & 3])
+    take(mb.at[pl.ds(0, 15)], mb_r.at[0])
     for quad in range(4):
         got = mb[pl.ds(quad * 4, 4), 0 : ROWS + 1]
         total = total + ((got[0] + got[1]) + (got[2] + got[3]))
@@ -383,7 +382,7 @@
             dma((1,)), dma((5,)), dma((3,)),
             dma((1,)), dma((1,)),
             dma((1,)), dma((1,)),
-            dma((1,)), dma((4,)),
+            dma((1,)), dma((1,)),
         ],
         compiler_params=pltpu.CompilerParams(
             collective_id=0, has_side_effects=True, vmem_limit_bytes=40 * 2**20

time: 46.8 us -> 46.8 us (level)
  no operation moved by 1% of the time
where the time goes in v8:
time: 46.8 us; the launch traced here: 46.6 us
  Pallas kernels  46 us (98%)
  between operations  0.64 us (1%)
    pallas_call x1, Pallas kernels, shards(): pl.pallas_call(kernel, name='sinkhorn', out_shape=tuple((pltpu.VMEM(v.sha...  45.4 us

profile of v8, /device:TPU:1, one launch (start us, length us, event | category | flops | bytes accessed | tf_op | source)
XLA Modules:
  0.0 46.6 jit_solution(6739299476782264792)
XLA Ops:
  0.6 45.4 %sinkhorn.1 = (f32[1,64]{1,0:T(1,128)S(1)}, f32[4,128]{1,0:T(4,128)S(1)}, f32[64,128]{1,0:T(8,128)S(1)}) custom-call(f32[64,128]{1,0:T(8,128)} %ps.1, f32[512,128]{1,0:T(8,128)} %pt.1, f32[1,64]{1,0:T(1,128)} %bitcast.7, f32[4,128]{1,0:T(4,128)} %bitcast.5, f32[4,128]{1,0:T(4,128)} %bitcast.6), custom_call_target="tpu_custom_call" | custom-call | tf_op jit(solution)/shard_map/sinkhorn/pallas_call | solution.py:349
  46.0 0.6 %finish.1 = (f32[1,64]{1,0:T(1,128)}, f32[4,128]{1,0:T(4,128)}, f32[64,128]{1,0:T(8,128)}) custom-call(f32[1,64]{1,0:T(1,128)S(1)} %get-tuple-element.9.f_ref, f32[4,128]{1,0:T(4,128)S(1)} %get-tuple-element.10.t_ref, f32[64,128]{1,0:T(8,128)S(1)} %get-tuple-element.11.m_ref), custom_call_target="tpu_custom_call" | custom-call | tf_op jit(solution)/shard_map/finish/pallas_call | solution.py:402
